TPU v7x, 32 devices: a whole 2x2x4 slice. The times are simulated.
32 devices in a mesh: replica: 2 (over y), fsdp: 4 (over x, core), seq: 4 (over z).
Axes of the slice: x: 2, y: 2, z: 4, core: 2. Of those that a mesh axis runs over, the one named last changes fastest.
Arguments:
- tokens: bfloat16 [8, 1024, 768], P(('replica', 'fsdp'), 'seq'), may hold values from -6 to 6
- cotangent: bfloat16 [8, 1024, 768], P(('replica', 'fsdp'), 'seq'), may hold values from -6 to 6
- expert_ids: int32 [8, 1024, 1], P(('replica', 'fsdp'), 'seq'), may hold values from 0 to 3; in each aligned block of 256 rows (0 to 255, 256 to 511, ..., all dimensions but the last counted through in order) at most 80 rows name the same one
- attn_gain: bfloat16 [768], P(('fsdp', 'seq')), may hold values from 0.5 to 1.5
- qkv_weight: bfloat16 [768, 2304], P(('fsdp', 'seq')), may hold values from -0.21875 to 0.21875
- output_weight: bfloat16 [768, 768], P(('fsdp', 'seq')), may hold values from -4 to 4
- bias_table: bfloat16 [384], P(('fsdp', 'seq')), may hold values from -4 to 4
- ffn_gain: bfloat16 [768], P(('fsdp', 'seq')), may hold values from 0.5 to 1.5
- router_projection_weight: bfloat16 [768, 4], P(('fsdp', 'seq')), may hold values from -0.15625 to 0.15625
- expert_in: bfloat16 [3072, 4, 768], P(('fsdp', 'seq')), may hold values from -0.21875 to 0.21875
- expert_out: bfloat16 [3072, 4, 768], P(('fsdp', 'seq')), may hold values from -0.4375 to 0.4375
Outputs:
- layer_out: bfloat16 [8, 1024, 768], P(('replica', 'fsdp'), 'seq')
- grad_tokens: bfloat16 [8, 1024, 768], P(('replica', 'fsdp'), 'seq')
- grad_attn_gain: float32 [768], P(('fsdp', 'seq'))
- grad_qkv_weight: float32 [768, 2304], P(('fsdp', 'seq'))
- grad_output_weight: float32 [768, 768], P(('fsdp', 'seq'))
- grad_bias_table: float32 [384], P(('fsdp', 'seq'))
- grad_ffn_gain: float32 [768], P(('fsdp', 'seq'))
- grad_router_weight: float32 [768, 4], P(('fsdp', 'seq'))
- grad_expert_in: float32 [3072, 4, 768], P(('fsdp', 'seq'))
- grad_expert_out: float32 [3072, 4, 768], P(('fsdp', 'seq'))
Inputs may be any that keep to these rules, and one draw needn't show every extreme that they name: `expert_ids`: in each aligned block of 256 positions of a sequence no expert is named by more than 80 tokens, and in every draw some block has an expert named by exactly 80.
All inputs are finite; a program needn't handle non-finite values.
Results may differ from a plain program's by a relative error of at most 0.017.
Values may be sent and summed in bfloat16 or wider, within the bound.
No kernel may reach another device: no remote copies, remote signals or barrier semaphores. Data moves between devices by JAX's collectives and lax.ppermute only.
A program may use at most 192 MiB of HBM per device.

v0:
```python
import jax
import jax.numpy as jnp
from jax import lax
from jax.sharding import PartitionSpec as P

HEADS = 12
HEAD_DIM = 64
BUCKETS = 32
EXPERTS = 4


epsilon = 1e-06
top_expert_index = lax.Precision.HIGHEST
thresholds = (12, 16, 23, 32, 46, 64, 91)
score_scale = 0.125
far_below = -1e30


def smooth_unit(values):
    return (
        0.5
        * values
        * (1.0 + jnp.tanh(0.7978845608028654 * (values + 0.044715 * values * values * values)))
    )


def bucket_of(distance):
    magnitude = jnp.abs(distance)
    far_bucket = jnp.full(distance.shape, 8, jnp.int32)
    for boundary in thresholds:
        far_bucket = far_bucket + (magnitude >= boundary).astype(jnp.int32)
    bucket_near = jnp.where(magnitude < 8, magnitude, far_bucket)
    return bucket_near + 16 * (distance > 0).astype(jnp.int32)


def bucket_pick(first_gap, span_len):
    gap_values = first_gap + jnp.arange(span_len, dtype=jnp.int32)
    return (bucket_of(gap_values)[:, None] == jnp.arange(BUCKETS, dtype=jnp.int32)[None, :]).astype(
        jnp.float32
    )


def expand_diagonals(diag_bias, count_q, count_k):
    head_count, span_len = diag_bias.shape
    flattened = jnp.broadcast_to(diag_bias[:, None, :], (head_count, count_q, span_len)).reshape(
        head_count, count_q * span_len
    )
    trimmed = flattened[:, : count_q * (span_len - 1)].reshape(head_count, count_q, span_len - 1)
    return trimmed[:, :, count_q - 1 : count_q - 1 + count_k]


def fold_diagonals(upstream_gradient):
    head_count, count_q, count_k = upstream_gradient.shape
    span_len = count_q + count_k
    placed = jnp.pad(upstream_gradient, ((0, 0), (0, 0), (count_q - 1, 0))).reshape(
        head_count, count_q * (span_len - 1)
    )
    placed = jnp.pad(placed, ((0, 0), (0, count_q))).reshape(head_count, count_q, span_len)
    return jnp.sum(placed, axis=1)


def block_scores(queries, key_blk, bias_grid, first_gap):
    token_row_count = queries.shape[1]
    key_count = key_blk.shape[1]
    bucket_hot = bucket_pick(first_gap, token_row_count + key_count)
    diag_bias = jnp.einsum("tb,bh->ht", bucket_hot, bias_grid, precision=top_expert_index)
    bias_block = expand_diagonals(diag_bias, token_row_count, key_count)
    scores = jnp.einsum("sqhd,skhd->shqk", queries, key_blk, preferred_element_type=jnp.float32)
    return (scores * score_scale + bias_block[None], bucket_hot)


def norm_back(upstream_gradient, unit_rows, inv_scale, gain_row):
    scaled = upstream_gradient * gain_row
    gain_grad = jnp.sum(upstream_gradient * unit_rows, axis=(0, 1))
    inner = jnp.mean(scaled * unit_rows, axis=-1, keepdims=True)
    return (inv_scale * (scaled - unit_rows * inner), gain_grad)


def per_device(
    tokens,
    cotangent,
    expert_ids,
    attn_gain,
    qkv_weight,
    output_weight,
    bias_table,
    ffn_gain,
    router_projection_weight,
    expert_in,
    expert_out,
):
    seq_count, token_row_count, model_width = tokens.shape
    slot_count = token_row_count * 5 // (4 * EXPERTS)
    length = token_row_count * lax.axis_size("seq")
    offset = lax.axis_index("seq") * token_row_count
    dense_full = (
        lax.all_gather(attn_gain, ("fsdp", "seq"), axis=0, tiled=True),
        lax.all_gather(qkv_weight, ("fsdp", "seq"), axis=0, tiled=True),
        lax.all_gather(output_weight, ("fsdp", "seq"), axis=0, tiled=True),
        lax.all_gather(bias_table, ("fsdp", "seq"), axis=0, tiled=True),
        lax.all_gather(ffn_gain, ("fsdp", "seq"), axis=0, tiled=True),
        lax.all_gather(router_projection_weight, ("fsdp", "seq"), axis=0, tiled=True),
    )
    bias_grid = dense_full[3].astype(jnp.float32).reshape(BUCKETS, HEADS)
    inputs = tokens.astype(jnp.float32)
    scale_one = lax.rsqrt(jnp.mean(inputs * inputs, axis=-1, keepdims=True) + epsilon)
    unit_one = inputs * scale_one
    normed_one = (unit_one * dense_full[0].astype(jnp.float32)).astype(jnp.bfloat16)
    projected = jnp.einsum(
        "std,de->ste", normed_one, dense_full[1], preferred_element_type=jnp.float32
    ).astype(jnp.bfloat16)
    queries = projected[:, :, :model_width].reshape(seq_count, token_row_count, HEADS, HEAD_DIM)
    key_rows = projected[:, :, model_width : 2 * model_width]
    value_rows = projected[:, :, 2 * model_width :]
    keys_front, values_front = (
        lax.all_gather(key_rows, "seq", axis=1, tiled=True),
        lax.all_gather(value_rows, "seq", axis=1, tiled=True),
    )
    block_len = 512
    block_count = length // block_len

    def stat_block(state, block_index):
        running_max, denominator = state
        first_key = block_index * block_len
        key_blk = lax.dynamic_slice_in_dim(keys_front, first_key, block_len, 1).reshape(
            seq_count, block_len, HEADS, HEAD_DIM
        )
        scores, bucket_hot = block_scores(
            queries, key_blk, bias_grid, first_key - offset - (token_row_count - 1)
        )
        new_max = jnp.maximum(running_max, jnp.max(scores, axis=-1))
        denominator = denominator * jnp.exp(running_max - new_max) + jnp.sum(
            jnp.exp(scores - new_max[..., None]), axis=-1
        )
        return ((new_max, denominator), None)

    stat_init = (
        jnp.full((seq_count, HEADS, token_row_count), far_below, jnp.float32),
        jnp.zeros((seq_count, HEADS, token_row_count), jnp.float32),
    )
    stat_final, unused = lax.scan(stat_block, stat_init, jnp.arange(block_count, dtype=jnp.int32))
    log_total = stat_final[0] + jnp.log(stat_final[1])

    def value_block(numerator, block_index):
        first_key = block_index * block_len
        key_blk = lax.dynamic_slice_in_dim(keys_front, first_key, block_len, 1).reshape(
            seq_count, block_len, HEADS, HEAD_DIM
        )
        value_blk = lax.dynamic_slice_in_dim(values_front, first_key, block_len, 1).reshape(
            seq_count, block_len, HEADS, HEAD_DIM
        )
        scores, bucket_hot = block_scores(
            queries, key_blk, bias_grid, first_key - offset - (token_row_count - 1)
        )
        weights = jnp.exp(scores - log_total[..., None]).astype(jnp.bfloat16)
        return (
            numerator
            + jnp.einsum("shqk,skhd->sqhd", weights, value_blk, preferred_element_type=jnp.float32),
            None,
        )

    mixed_float, unused = lax.scan(
        value_block,
        jnp.zeros((seq_count, token_row_count, HEADS, HEAD_DIM), jnp.float32),
        jnp.arange(block_count, dtype=jnp.int32),
    )
    mixed = mixed_float.reshape(seq_count, token_row_count, model_width).astype(jnp.bfloat16)
    branch = jnp.einsum("std,de->ste", mixed, dense_full[2], preferred_element_type=jnp.float32)
    hidden = inputs + branch
    second_norm_scale = lax.rsqrt(jnp.mean(hidden * hidden, axis=-1, keepdims=True) + epsilon)
    unit_two = hidden * second_norm_scale
    second_normed_input = (unit_two * dense_full[4].astype(jnp.float32)).astype(jnp.bfloat16)
    router_logits = jnp.einsum(
        "std,de->ste", second_normed_input, dense_full[5], preferred_element_type=jnp.float32
    )
    raised = jnp.exp(router_logits - jnp.max(router_logits, axis=-1, keepdims=True))
    chances = raised / jnp.sum(raised, axis=-1, keepdims=True)
    routes = expert_ids[..., 0]
    chosen_int = (routes[..., None] == jnp.arange(EXPERTS, dtype=jnp.int32)).astype(jnp.int32)
    chosen = chosen_int.astype(jnp.float32)
    gating = jnp.sum(chances * chosen, axis=-1)
    slot_index = jnp.sum((jnp.cumsum(chosen_int, axis=1) - chosen_int) * chosen_int, axis=-1)
    target = routes * slot_count + slot_index
    dispatch = (target[..., None] == jnp.arange(EXPERTS * slot_count, dtype=jnp.int32)).astype(
        jnp.bfloat16
    )
    expert_rows = (
        jnp.einsum(
            "stc,std->scd", dispatch, second_normed_input, preferred_element_type=jnp.float32
        )
        .astype(jnp.bfloat16)
        .reshape(seq_count, EXPERTS, slot_count, model_width)
    )
    piece_in = lax.all_gather(expert_in, ("fsdp", "seq"), axis=0, tiled=True)
    piece_out = lax.all_gather(expert_out, ("fsdp", "seq"), axis=0, tiled=True)
    pre_act = jnp.einsum(
        "secd,fed->secf", expert_rows, piece_in, preferred_element_type=jnp.float32
    )
    activation = smooth_unit(pre_act).astype(jnp.bfloat16)
    expert_sum = jnp.einsum(
        "secf,fed->secd", activation, piece_out, preferred_element_type=jnp.float32
    )
    expert_result = expert_sum.astype(jnp.bfloat16).reshape(
        seq_count, EXPERTS * slot_count, model_width
    )
    combined = jnp.einsum(
        "stc,scd->std", dispatch, expert_result, preferred_element_type=jnp.float32
    )
    layer_out = (hidden + gating[..., None] * combined).astype(jnp.bfloat16)
    dense_again = (
        lax.all_gather(attn_gain, ("fsdp", "seq"), axis=0, tiled=True),
        lax.all_gather(qkv_weight, ("fsdp", "seq"), axis=0, tiled=True),
        lax.all_gather(output_weight, ("fsdp", "seq"), axis=0, tiled=True),
        lax.all_gather(bias_table, ("fsdp", "seq"), axis=0, tiled=True),
        lax.all_gather(ffn_gain, ("fsdp", "seq"), axis=0, tiled=True),
        lax.all_gather(router_projection_weight, ("fsdp", "seq"), axis=0, tiled=True),
    )
    grad_out = cotangent.astype(jnp.float32)
    gate_grad = jnp.sum(grad_out * combined, axis=-1)
    slot_grad = (gating[..., None] * grad_out).astype(jnp.bfloat16)
    result_grad = (
        jnp.einsum("stc,std->scd", dispatch, slot_grad, preferred_element_type=jnp.float32)
        .astype(jnp.bfloat16)
        .reshape(seq_count, EXPERTS, slot_count, model_width)
    )
    piece_in = lax.all_gather(expert_in, ("fsdp", "seq"), axis=0, tiled=True)
    piece_out = lax.all_gather(expert_out, ("fsdp", "seq"), axis=0, tiled=True)
    pre_act = jnp.einsum(
        "secd,fed->secf", expert_rows, piece_in, preferred_element_type=jnp.float32
    )
    act_grad = jnp.einsum(
        "secd,fed->secf", result_grad, piece_out, preferred_element_type=jnp.float32
    )
    activation, pullback = jax.vjp(smooth_unit, pre_act)
    pre_grad = pullback(act_grad)[0].astype(jnp.bfloat16)
    rows_grad = jnp.einsum("secf,fed->secd", pre_grad, piece_in, preferred_element_type=jnp.float32)
    normed_grad = jnp.einsum(
        "stc,scd->std",
        dispatch.astype(jnp.float32),
        rows_grad.reshape(seq_count, EXPERTS * slot_count, model_width),
        precision=top_expert_index,
    )
    logit_grad = (gate_grad * gating)[..., None] * (chosen - chances)
    normed_grad = normed_grad + jnp.einsum(
        "ste,de->std", logit_grad, dense_again[5].astype(jnp.float32), precision=top_expert_index
    )
    router_grad = jnp.einsum(
        "std,ste->de",
        second_normed_input.astype(jnp.float32),
        logit_grad,
        precision=top_expert_index,
    )
    hidden_grad, gain_two_grad = norm_back(
        normed_grad, unit_two, second_norm_scale, dense_again[4].astype(jnp.float32)
    )
    hidden_grad = grad_out + hidden_grad
    hidden_low = hidden_grad.astype(jnp.bfloat16)
    out_weight_grad = jnp.einsum(
        "std,ste->de", mixed, hidden_low, preferred_element_type=jnp.float32
    )
    mixed_grad = jnp.einsum(
        "ste,de->std", hidden_low, dense_again[2], preferred_element_type=jnp.float32
    ).astype(jnp.bfloat16)
    keys_all, values_all = (
        lax.all_gather(key_rows, "seq", axis=1, tiled=True),
        lax.all_gather(value_rows, "seq", axis=1, tiled=True),
    )
    grad_heads = mixed_grad.reshape(seq_count, token_row_count, HEADS, HEAD_DIM)
    row_dot = jnp.einsum(
        "sqhd,sqhd->shq", grad_heads.astype(jnp.float32), mixed_float, precision=top_expert_index
    )
    bias_back = dense_again[3].astype(jnp.float32).reshape(BUCKETS, HEADS)

    def back_block(state, block_index):
        query_grad, bias_grad, key_value_grad = state
        first_key = block_index * block_len
        key_blk = lax.dynamic_slice_in_dim(keys_all, first_key, block_len, 1).reshape(
            seq_count, block_len, HEADS, HEAD_DIM
        )
        value_blk = lax.dynamic_slice_in_dim(values_all, first_key, block_len, 1).reshape(
            seq_count, block_len, HEADS, HEAD_DIM
        )
        scores, bucket_hot = block_scores(
            queries, key_blk, bias_back, first_key - offset - (token_row_count - 1)
        )
        weights = jnp.exp(scores - log_total[..., None])
        prob_grad = jnp.einsum(
            "sqhd,skhd->shqk", grad_heads, value_blk, preferred_element_type=jnp.float32
        )
        score_float = weights * (prob_grad - row_dot[..., None])
        score_grad = score_float.astype(jnp.bfloat16)
        query_grad = (
            query_grad
            + jnp.einsum("shqk,skhd->sqhd", score_grad, key_blk, preferred_element_type=jnp.float32)
            * score_scale
        )
        key_grad = (
            jnp.einsum("shqk,sqhd->skhd", score_grad, queries, preferred_element_type=jnp.float32)
            * score_scale
        )
        value_grad = jnp.einsum(
            "shqk,sqhd->skhd",
            weights.astype(jnp.bfloat16),
            grad_heads,
            preferred_element_type=jnp.float32,
        )
        diag_grad = fold_diagonals(jnp.sum(score_float, axis=0))
        bias_grad = bias_grad + jnp.einsum(
            "tb,ht->bh", bucket_hot, diag_grad, precision=top_expert_index
        )
        kv_pair = jnp.concatenate(
            [
                key_grad.reshape(seq_count, block_len, model_width),
                value_grad.reshape(seq_count, block_len, model_width),
            ],
            axis=-1,
        )
        key_value_grad = lax.dynamic_update_slice_in_dim(key_value_grad, kv_pair, first_key, 1)
        return ((query_grad, bias_grad, key_value_grad), None)

    back_state = (
        jnp.zeros((seq_count, token_row_count, HEADS, HEAD_DIM), jnp.float32),
        jnp.zeros((BUCKETS, HEADS), jnp.float32),
        jnp.zeros((seq_count, length, 2 * model_width), jnp.float32),
    )
    back_final, unused = lax.scan(back_block, back_state, jnp.arange(block_count, dtype=jnp.int32))
    query_grad, bias_grad, key_value_grad = back_final
    own_kv_grad = lax.psum_scatter(
        key_value_grad.astype(jnp.bfloat16), "seq", scatter_dimension=1, tiled=True
    ).astype(jnp.float32)
    projected_grad = jnp.concatenate(
        [query_grad.reshape(seq_count, token_row_count, model_width), own_kv_grad], axis=-1
    ).astype(jnp.bfloat16)
    qkv_grad = jnp.einsum(
        "std,ste->de", normed_one, projected_grad, preferred_element_type=jnp.float32
    )
    normed_one_grad = jnp.einsum(
        "ste,de->std", projected_grad, dense_again[1], preferred_element_type=jnp.float32
    )
    input_grad, gain_one_grad = norm_back(
        normed_one_grad, unit_one, scale_one, dense_again[0].astype(jnp.float32)
    )
    input_grad = (hidden_grad + input_grad).astype(jnp.bfloat16)
    dense_shards = (
        lax.psum_scatter(gain_one_grad, ("fsdp", "seq"), scatter_dimension=0, tiled=True),
        lax.psum_scatter(qkv_grad, ("fsdp", "seq"), scatter_dimension=0, tiled=True),
        lax.psum_scatter(out_weight_grad, ("fsdp", "seq"), scatter_dimension=0, tiled=True),
        lax.psum_scatter(
            bias_grad.reshape(BUCKETS * HEADS), ("fsdp", "seq"), scatter_dimension=0, tiled=True
        ),
        lax.psum_scatter(gain_two_grad, ("fsdp", "seq"), scatter_dimension=0, tiled=True),
        lax.psum_scatter(router_grad, ("fsdp", "seq"), scatter_dimension=0, tiled=True),
    )
    rows_piece = lax.all_gather(expert_rows, ("fsdp", "seq"), axis=0, tiled=True)
    grad_piece = lax.all_gather(result_grad, ("fsdp", "seq"), axis=0, tiled=True)
    pre_act = jnp.einsum(
        "secd,fed->secf", rows_piece, expert_in, preferred_element_type=jnp.float32
    )
    act_grad = jnp.einsum(
        "secd,fed->secf", grad_piece, expert_out, preferred_element_type=jnp.float32
    )
    activation, pullback = jax.vjp(smooth_unit, pre_act)
    pre_grad = pullback(act_grad)[0].astype(jnp.bfloat16)
    in_total = jnp.einsum(
        "secf,secd->fed", pre_grad, rows_piece, preferred_element_type=jnp.float32
    )
    out_total = jnp.einsum(
        "secf,secd->fed",
        activation.astype(jnp.bfloat16),
        grad_piece,
        preferred_element_type=jnp.float32,
    )
    summed = (
        lax.psum(dense_shards[0].astype(jnp.bfloat16), "replica").astype(jnp.float32),
        lax.psum(dense_shards[1].astype(jnp.bfloat16), "replica").astype(jnp.float32),
        lax.psum(dense_shards[2].astype(jnp.bfloat16), "replica").astype(jnp.float32),
        lax.psum(dense_shards[3].astype(jnp.bfloat16), "replica").astype(jnp.float32),
        lax.psum(dense_shards[4].astype(jnp.bfloat16), "replica").astype(jnp.float32),
        lax.psum(dense_shards[5].astype(jnp.bfloat16), "replica").astype(jnp.float32),
        lax.psum(jnp.stack([in_total, out_total], axis=1).astype(jnp.bfloat16), "replica").astype(
            jnp.float32
        ),
    )
    expert_total = summed[6]
    return (
        layer_out,
        input_grad,
        summed[0],
        summed[1],
        summed[2],
        summed[3],
        summed[4],
        summed[5],
        expert_total[:, 0],
        expert_total[:, 1],
    )


def solution(mesh):
    return jax.shard_map(
        per_device,
        mesh=mesh,
        in_specs=(
            P(("replica", "fsdp"), "seq", None),
            P(("replica", "fsdp"), "seq", None),
            P(("replica", "fsdp"), "seq", None),
            P(("fsdp", "seq")),
            P(("fsdp", "seq"), None),
            P(("fsdp", "seq"), None),
            P(("fsdp", "seq")),
            P(("fsdp", "seq")),
            P(("fsdp", "seq"), None),
            P(("fsdp", "seq"), None, None),
            P(("fsdp", "seq"), None, None),
        ),
        out_specs=(
            P(("replica", "fsdp"), "seq", None),
            P(("replica", "fsdp"), "seq", None),
            P(("fsdp", "seq")),
            P(("fsdp", "seq"), None),
            P(("fsdp", "seq"), None),
            P(("fsdp", "seq")),
            P(("fsdp", "seq")),
            P(("fsdp", "seq"), None),
            P(("fsdp", "seq"), None, None),
            P(("fsdp", "seq"), None, None),
        ),
        check_vma=False,
    )
```

profile of v0, /device:TPU:0, one launch (start us, length us, event | category | flops | bytes accessed | tf_op | source)
XLA Modules:
  0.0 1366.2 jit_solution(10179174713592509193)
XLA Ops:
  13.1 36.9 %all-reduce.9 = (bf16[384]{0:T(512)(128)(2,1)S(1)}, bf16[768]{0:T(1024)(128)(2,1)S(1)}, bf16[768]{0:T(1024)(128)(2,1)S(1)}) all-reduce(bf16[384]{0:T(512)(128)(2,1)S(1)} %dynamic-update-slice.1, bf16[768]{0:T(1024)(128)(2,1)S(1)} %dynamic-update-slice, ...), channel_id=1, replica_groups=mesh['replica'=2,'fsdp'=4,'seq'=4] {'fsdp','seq'}, use_global_device_ids=true, to_apply=%add.3 | all-reduce | flops 1920 | bytes 7680
  51.3 9.0 all-gather.10.cloned.1.call-done
  71.5 31.2 %all-gather = bf16[16,48,4]{1,2,0:T(4,128)(2,1)S(1)} all-gather(bf16[1,48,4]{1,2,0:T(4,128)(2,1)S(1)} %bitcast.490), channel_id=1, replica_groups=mesh['replica'=2,'fsdp'=4,'seq'=4] {'fsdp','seq'}, dimensions={0}, use_global_device_ids=true | all-gather | bytes 6528 | tf_op jit(solution)/shard_map/all_gather | solution.py:102
  106.8 32.6 %all-gather.14.cloned.1.call-done = bf16[1,1024,768]{2,1,0:T(8,128)(2,1)} async-done(((bf16[1,256,768]{2,1,0:T(8,128)(2,1)}), bf16[1,1024,768]{2,1,0:T(8,128)(2,1)}) %all-gather.14.cloned.1.call-update) | async-done | bytes 1572880 | tf_op jit(solution)/shard_map/all_gather | solution.py:116
  141.1 176.6 %while.45 = (s32[]{:T(128)}, f32[1,12,256]{2,1,0:T(8,128)S(1)}, f32[1,12,256]{2,1,0:T(8,128)S(1)}, s32[2]{0:T(128)S(1)}, bf16[1,1024,768]{1,2,0:T(8,128)(2,1)S(1...) while((s32[]{:T(128)}, f32[1,12,256]{2,1,0:T(8,128)S(1)}, ...), condition=%wide.region_4.5_spmd.clone, body=%wide.region_1.4_spmd.clone.sunk | while | flops 212791296 | bytes 141356800 | solution.py:141
  150.2 16.4 %copy.176 = f32[2,8,256,768]{3,1,2,0:T(8,128)} copy(f32[2,8,256,768]{3,2,1,0:T(8,128)} %bitcast.443) | data formatting | bytes 25165824 | tf_op jit(solution)/shard_map/while
  166.6 10.1 slice.97
  176.7 20.2 %reshape.856 = f32[12,256,767]{2,1,0:T(8,128)} reshape(f32[12,196352]{1,0:T(8,128)} %slice.97) | data formatting | bytes 18849792 | tf_op jit(solution)/shard_map/while/body/eval_jaxpr/reshape | solution.py:48
  196.9 7.7 slice.98
  230.4 16.6 %copy.176 = f32[2,8,256,768]{3,1,2,0:T(8,128)} copy(f32[2,8,256,768]{3,2,1,0:T(8,128)} %bitcast.443) | data formatting | bytes 25165824 | tf_op jit(solution)/shard_map/while
  247.0 10.3 slice.97
  257.3 20.3 %reshape.856 = f32[12,256,767]{2,1,0:T(8,128)} reshape(f32[12,196352]{1,0:T(8,128)} %slice.97) | data formatting | bytes 18849792 | tf_op jit(solution)/shard_map/while/body/eval_jaxpr/reshape | solution.py:48
  318.3 156.4 %while.46 = (s32[]{:T(128)}, f32[1,256,12,64]{1,3,2,0:T(8,128)}, s32[2]{0:T(128)S(1)}, bf16[1,1024,768]{1,2,0:T(8,128)(2,1)}, bf16[1,1024,768]{1,2,0:T(8,128)(2,...) while((s32[]{:T(128)}, f32[1,256,12,64]{1,3,2,0:T(8,128)}, ...), condition=%wide.region_6.7_spmd.clone, body=%wide.region_5.6_spmd.clone.sunk | while | flops 412922880 | bytes 132558584 | solution.py:162
  329.3 16.6 %copy.178 = f32[2,8,256,768]{3,1,2,0:T(8,128)} copy(f32[2,8,256,768]{3,2,1,0:T(8,128)} %bitcast.444) | data formatting | bytes 25165824 | tf_op jit(solution)/shard_map/while
  345.9 10.3 slice.99
  356.2 20.4 %reshape.857 = f32[12,256,767]{2,1,0:T(8,128)} reshape(f32[12,196352]{1,0:T(8,128)} %slice.99) | data formatting | bytes 18849792 | tf_op jit(solution)/shard_map/while/body/eval_jaxpr/reshape | solution.py:48
  376.5 7.7 slice.100
  407.6 16.4 %copy.178 = f32[2,8,256,768]{3,1,2,0:T(8,128)} copy(f32[2,8,256,768]{3,2,1,0:T(8,128)} %bitcast.444) | data formatting | bytes 25165824 | tf_op jit(solution)/shard_map/while
  424.0 10.1 slice.99
  434.1 20.1 %reshape.857 = f32[12,256,767]{2,1,0:T(8,128)} reshape(f32[12,196352]{1,0:T(8,128)} %slice.99) | data formatting | bytes 18849792 | tf_op jit(solution)/shard_map/while/body/eval_jaxpr/reshape | solution.py:48
  482.8 14.2 %convolution_bitcast_fusion.4 = f32[1,4,80,3072]{3,2,1,0:T(8,128)} fusion(bf16[4,80,768]{2,1,0:T(8,128)(2,1)} %bitcast.464, bf16[3072,4,768]{2,0,1:T(8,128)(2,1)} %all-gather.18.cloned.1.call-done), kind=kOutput, calls=%fused_computation.113 | convolution fusion | flops 1509949440 | bytes 23298048 | tf_op jit(solution)/shard_map/secd,fed->secf/dot_general | solution.py:196
  497.0 17.7 %fusion.100 = f32[4,80,768]{2,1,0:T(8,128)} fusion(bf16[3072,4,768]{2,0,1:T(8,128)(2,1)} %all-gather.18.cloned.1.call-done, f32[1,4,80,3072]{3,2,1,0:T(8,128)} %convolution_bitcast_fusion.4, bf16[4,80,768]{2,1,0:T(8,128)(2,1)} %bitcast.468, bf16[3072,4,768]{2,0,1:T(8,128)(2,1)} %all-gather.20.cloned.1.call-done), kind=kOutput, calls=%fused_computation.136 | convolution fusion | flops 3043491840 | bytes 43155456 | tf_op jit(solution)/shard_map/secf,fed->secd/dot_general | solution.py:236
  516.9 11.1 fusion.113
  536.0 309.6 %while.47 = (s32[]{:T(128)}, f32[1,256,12,64]{1,3,2,0:T(8,128)}, f32[32,12]{0,1:T(8,128)S(1)}, bf16[1,1024,1536]{1,2,0:T(8,128)(2,1)}, s32[2]{0:T(128)S(1)}, /*i...) while((s32[]{:T(128)}, f32[1,256,12,64]{1,3,2,0:T(8,128)}, ...), condition=%wide.region_18.19_spmd.clone, body=%wide.region_16.18_spmd.clone.sunk | while | flops 1033237248 | bytes 390944992 | solution.py:326
  546.4 16.4 %copy.180 = f32[2,8,256,768]{3,1,2,0:T(8,128)} copy(f32[2,8,256,768]{3,2,1,0:T(8,128)} %bitcast.446) | data formatting | bytes 25165824 | tf_op jit(solution)/shard_map/while
  562.8 10.3 slice.102
  573.1 20.1 %reshape.858 = f32[12,256,767]{2,1,0:T(8,128)} reshape(f32[12,196352]{1,0:T(8,128)} %slice.102) | data formatting | bytes 18849792 | tf_op jit(solution)/shard_map/while/body/eval_jaxpr/reshape | solution.py:48
  627.4 8.6 pad.14.clone.2
  636.1 16.5 %reshape.859 = f32[12,196352]{1,0:T(8,128)} reshape(f32[12,256,767]{2,1,0:T(8,128)} %pad.14.clone.2) | data formatting | bytes 18849792 | tf_op jit(solution)/shard_map/while/body/eval_jaxpr/reshape | solution.py:55
  652.6 10.2 pad.50
  662.8 13.0 copy.183
  697.4 16.4 %copy.180 = f32[2,8,256,768]{3,1,2,0:T(8,128)} copy(f32[2,8,256,768]{3,2,1,0:T(8,128)} %bitcast.446) | data formatting | bytes 25165824 | tf_op jit(solution)/shard_map/while
  713.8 10.5 slice.102
  724.2 20.1 %reshape.858 = f32[12,256,767]{2,1,0:T(8,128)} reshape(f32[12,196352]{1,0:T(8,128)} %slice.102) | data formatting | bytes 18849792 | tf_op jit(solution)/shard_map/while/body/eval_jaxpr/reshape | solution.py:48
  778.3 8.6 pad.14.clone.2
  787.0 16.5 %reshape.859 = f32[12,196352]{1,0:T(8,128)} reshape(f32[12,256,767]{2,1,0:T(8,128)} %pad.14.clone.2) | data formatting | bytes 18849792 | tf_op jit(solution)/shard_map/while/body/eval_jaxpr/reshape | solution.py:55
  803.5 10.3 pad.50
  813.7 13.0 copy.183
  849.2 55.9 %reduce-scatter.7.cloned.1.call-done = bf16[1,256,1536]{1,2,0:T(8,128)(2,1)} async-done(((bf16[1,1024,1536]{1,2,0:T(8,128)(2,1)}), bf16[1,256,1536]{1,2,0:T(8,128)(2,1)}) %reduce-scatter.7.cloned.1.call-update) | async-done | bytes 786448 | tf_op jit(solution)/shard_map/reduce_scatter | solution.py:328
  910.5 68.7 %all-gather.22.cloned.1.call-done = bf16[16,4,80,768]{3,2,0,1:T(8,128)(2,1)} async-done(((bf16[1,4,80,768]{3,2,0,1:T(8,128)(2,1)}), bf16[16,4,80,768]{3,2,0,1:T(8,128)(2,1)}) %all-gather.22.cloned.1.call-update) | async-done | bytes 7864336 | tf_op jit(solution)/shard_map/all_gather | solution.py:354
  979.2 7.8 fusion.123
  987.0 64.5 %all-gather.24.cloned.1.call-done = bf16[16,4,80,768]{3,2,0,1:T(8,128)(2,1)} async-done(((bf16[1,4,80,768]{3,2,0,1:T(8,128)(2,1)}), bf16[16,4,80,768]{3,2,0,1:T(8,128)(2,1)}) %all-gather.24.cloned.1.call-update) | async-done | bytes 7864336 | tf_op jit(solution)/shard_map/all_gather | solution.py:355
  1051.5 8.4 fusion.112
  1060.0 13.2 fusion.111
  1078.0 39.0 %reduce-scatter.11.cloned.1.call-done = f32[48,768]{1,0:T(8,128)} async-done(((f32[768,768]{1,0:T(8,128)}), f32[48,768]{1,0:T(8,128)}) %reduce-scatter.11.cloned.1.call-update) | async-done | bytes 147472 | tf_op jit(solution)/shard_map/reduce_scatter | solution.py:347
  1118.6 92.1 %reduce-scatter.9.cloned.1.call-done = f32[48,2304]{1,0:T(8,128)} async-done(((f32[768,2304]{1,0:T(8,128)}), f32[48,2304]{1,0:T(8,128)}) %reduce-scatter.9.cloned.1.call-update) | async-done | bytes 442384 | tf_op jit(solution)/shard_map/reduce_scatter | solution.py:346
  1213.9 55.8 %reduce-scatter.13.cloned.1.call-done = f32[48,4]{1,0:T(8,128)} async-done(((f32[768,4]{1,0:T(8,128)}), f32[48,4]{1,0:T(8,128)}) %reduce-scatter.13.cloned.1.call-update) | async-done | bytes 784
  1273.8 59.2 %all-reduce.8 = (bf16[768]{0:T(1024)(128)(2,1)S(1)}, bf16[384]{0:T(512)(128)(2,1)S(1)}, bf16[768]{0:T(1024)(128)(2,1)S(1)}) all-reduce(f32[768]{0:T(1024)S(1)} %get-tuple-element.656, f32[384]{0:T(512)S(1)} %reshape.799, f32[768]{0:T(1024)S(1)} %copy-done.45), channel_id=3, replica_groups=mesh['replica'=2,'fsdp'=4,'seq'=4] {'fsdp','seq'}, use_global_device_ids=true, to_apply=%region_22.23.clone | all-reduce | flops 1920 | bytes 11520
  (353 shorter events, 308.9 us)
Async XLA Ops:
  7.2 53.2 %all-gather.10.cloned.1.call-start = ((), (), s32[]{:S(2)}) async-start(), calls=%async_computation.4 | async-start | bytes 3760128 | tf_op jit(solution)/shard_map/all_gather | solution.py:98
  7.9 96.3 %all-gather.12.cloned.1.call-start = ((), (), s32[]{:S(2)}) async-start(), calls=%async_computation.5 | async-start | bytes 1966080 | tf_op jit(solution)/shard_map/all_gather | solution.py:117
  50.1 10.2 copy-start.28
  51.3 9.1 copy-start.43
  51.3 14.7 %copy-start.20 = (bf16[192,4,768]{2,1,0:T(4,128)(2,1)S(1)}, bf16[192,4,768]{2,1,0:T(4,128)(2,1)}, u32[]{:S(2)}) copy-start(bf16[192,4,768]{2,1,0:T(4,128)(2,1)} %param.26) | copy-start | bytes 3538948
  64.6 6.9 copy-start.56
  64.6 74.7 %all-gather.14.cloned.1.call-start = ((), (), s32[]{:S(2)}) async-start(), calls=%async_computation.6 | async-start | bytes 1966080 | tf_op jit(solution)/shard_map/all_gather | solution.py:116
  65.4 411.4 %all-gather.16.cloned.1.call-start = ((), (), s32[]{:S(2)}) async-start(), calls=%async_computation.7 | async-start | bytes 1253376 | tf_op jit(solution)/shard_map/all_gather | solution.py:99
  65.9 416.9 %all-gather.18.cloned.1.call-start = ((), (), s32[]{:S(2)}) async-start(), calls=%async_computation.8 | async-start | bytes 20054016 | tf_op jit(solution)/shard_map/all_gather | solution.py:194
  67.1 429.9 %all-gather.20.cloned.1.call-start = ((), (), s32[]{:S(2)}) async-start(), calls=%async_computation.9 | async-start | bytes 20054016 | tf_op jit(solution)/shard_map/all_gather | solution.py:195
  68.4 836.8 %reduce-scatter.7.cloned.1.call-start = ((), (), s32[]{:S(2)}) async-start(), calls=%async_computation.10 | async-start | bytes 3932160 | tf_op jit(solution)/shard_map/reduce_scatter | solution.py:328
  318.3 158.5 %copy-start.16 = (bf16[1,256,768]{2,1,0:T(8,128)(2,1)S(1)}, bf16[1,256,768]{2,1,0:T(8,128)(2,1)}, u32[]{:S(2)}) copy-start(bf16[1,256,768]{2,1,0:T(8,128)(2,1)} %param.17) | copy-start | bytes 1179652
  478.8 49.8 %copy-start.15 = (f32[1,256,768]{2,1,0:T(8,128)}, f32[1,256,768]{2,1,0:T(8,128)S(1)}, u32[]{:S(2)}) copy-start(f32[1,256,768]{2,1,0:T(8,128)S(1)} %get-tuple-element.747) | copy-start | bytes 2359300
  479.6 17.5 %copy-start.18 = (bf16[256,768]{1,0:T(8,128)(2,1)}, bf16[256,768]{1,0:T(8,128)(2,1)S(1)}, u32[]{:S(2)}) copy-start(bf16[256,768]{1,0:T(8,128)(2,1)S(1)} %fusion.142) | copy-start | bytes 1179652
  479.8 48.7 %copy-start.30 = (f32[256,4]{0,1:T(4,128)}, f32[256,4]{0,1:T(4,128)S(1)}, u32[]{:S(2)}) copy-start(f32[256,4]{0,1:T(4,128)S(1)} %get-tuple-element.749) | copy-start | bytes 12292
  497.0 17.7 %copy-start.42 = (s32[1,256,1]{1,2,0:T(1,128)S(1)}, s32[1,256,1]{1,2,0:T(1,128)}, u32[]{:S(2)}) copy-start(s32[1,256,1]{1,2,0:T(1,128)} %multiply_add_fusion.4) | copy-start | bytes 3076
  516.8 11.7 copy-start.47
  516.8 11.7 copy-start.36
  516.8 11.7 copy-start.39
  516.8 11.7 copy-start.49
  516.8 11.7 copy-start.52
  662.8 17.8 %slice-start.2 = ((s8[6291456]{0:T(1024)(128)(4,1)}), s8[4194304]{0:T(1024)(128)(4,1)S(1)}, s32[]{:S(2)}) async-start(s8[6291456]{0:T(1024)(128)(4,1)} %bitcast.441), calls=%async_computation.19 | async-start | bytes 8388608 | tf_op jit(solution)/shard_map/while
  662.8 17.8 %slice-start.3 = ((s8[6291456]{0:T(1024)(128)(4,1)}), s8[2097152]{0:T(1024)(128)(4,1)S(1)}, s32[]{:S(2)}) async-start(s8[6291456]{0:T(1024)(128)(4,1)} %bitcast.441), calls=%async_computation.20 | async-start | bytes 4194304 | tf_op jit(solution)/shard_map/while
  675.8 6.9 slice-start
  675.8 6.9 slice-start.1
  771.5 6.9 copy-start.9
  813.7 17.8 %slice-start.2 = ((s8[6291456]{0:T(1024)(128)(4,1)}), s8[4194304]{0:T(1024)(128)(4,1)S(1)}, s32[]{:S(2)}) async-start(s8[6291456]{0:T(1024)(128)(4,1)} %bitcast.441), calls=%async_computation.19 | async-start | bytes 8388608 | tf_op jit(solution)/shard_map/while
  813.7 17.8 %slice-start.3 = ((s8[6291456]{0:T(1024)(128)(4,1)}), s8[2097152]{0:T(1024)(128)(4,1)S(1)}, s32[]{:S(2)}) async-start(s8[6291456]{0:T(1024)(128)(4,1)} %bitcast.441), calls=%async_computation.20 | async-start | bytes 4194304 | tf_op jit(solution)/shard_map/while
  826.7 6.9 slice-start
  826.7 6.9 slice-start.1
  845.7 133.5 %all-gather.22.cloned.1.call-start = ((), (), s32[]{:S(2)}) async-start(), calls=%async_computation.13 | async-start | bytes 8355840 | tf_op jit(solution)/shard_map/all_gather | solution.py:354
  845.7 59.5 %copy-start.17 = (bf16[1,256,768]{2,1,0:T(8,128)(2,1)S(1)}, bf16[1,256,768]{2,1,0:T(8,128)(2,1)}, u32[]{:S(2)}) copy-start(bf16[1,256,768]{2,1,0:T(8,128)(2,1)} %param.17) | copy-start | bytes 1179652
  845.7 59.4 %copy-start.29 = (f32[768]{0:T(1024)S(1)}, f32[768]{0:T(1024)}, u32[]{:S(2)}) copy-start(f32[768]{0:T(1024)} %copy-done.28) | copy-start | bytes 9220
  845.7 59.4 %copy-start.44 = (f32[256]{0:T(256)S(1)}, f32[256]{0:T(256)}, u32[]{:S(2)}) copy-start(f32[256]{0:T(256)} %copy-done.43) | copy-start | bytes 3076
  846.4 205.1 %all-gather.24.cloned.1.call-start = ((), (), s32[]{:S(2)}) async-start(), calls=%async_computation.14 | async-start | bytes 8355840 | tf_op jit(solution)/shard_map/all_gather | solution.py:355
  847.2 269.9 %reduce-scatter.11.cloned.1.call-start = ((), (), s32[]{:S(2)}) async-start(), calls=%async_computation.12 | async-start | bytes 2506752 | tf_op jit(solution)/shard_map/reduce_scatter | solution.py:347
  849.1 361.5 %reduce-scatter.9.cloned.1.call-start = ((), (), s32[]{:S(2)}) async-start(), calls=%async_computation.11 | async-start | bytes 7520256 | tf_op jit(solution)/shard_map/reduce_scatter | solution.py:346
  910.4 68.7 %copy-start.21 = (bf16[192,4,768]{2,1,0:T(4,128)(2,1)S(1)}, bf16[192,4,768]{2,1,0:T(4,128)(2,1)}, u32[]{:S(2)}) copy-start(bf16[192,4,768]{2,1,0:T(4,128)(2,1)} %param.26) | copy-start | bytes 3538948
  910.5 359.2 %reduce-scatter.13.cloned.1.call-start = ((), (), s32[]{:S(2)}) async-start(), calls=%async_computation.15 | async-start | bytes 417792
  987.0 72.9 %copy-start.26 = (bf16[192,4,768]{2,1,0:T(4,128)(2,1)S(1)}, bf16[192,4,768]{2,1,0:T(4,128)(2,1)}, u32[]{:S(2)}) copy-start(bf16[192,4,768]{2,1,0:T(4,128)(2,1)} %param.27) | copy-start | bytes 3538948
  1059.9 13.2 copy-start.19
  1059.9 13.2 copy-start.31
  1059.9 13.2 copy-start.37
  1059.9 13.2 copy-start.40
  1059.9 13.2 copy-start.50
  1059.9 13.2 copy-start.54
  1074.5 196.0 %copy-start.27 = (bf16[1,256,1536]{1,2,0:T(8,128)(2,1)S(1)}, bf16[1,256,1536]{1,2,0:T(8,128)(2,1)}, u32[]{:S(2)}) copy-start(bf16[1,256,1536]{1,2,0:T(8,128)(2,1)} %reduce-scatter.7.cloned.1.call-done) | copy-start | bytes 2359300
  1074.5 273.5 %all-reduce.14.cloned.1.call-start = ((), (), s32[]{:S(2)}) async-start(), calls=%async_computation.16 | async-start | bytes 5308416 | tf_op jit(solution)/shard_map/psum | solution.py:375
  (41 other events, 135.6 us)
Sparse Core Ops, SparseCore 0:
  10.3 49.9 all-gather.9
  64.7 36.4 all-gather.11
  103.3 35.9 all-gather.13
  141.5 37.1 all-gather.15
  180.7 103.2 all-gather.17
  285.4 104.1 all-gather.19
  845.8 59.3 reduce-scatter.6
  907.5 71.6 all-gather.21
  981.5 69.9 all-gather.23
  1055.7 61.3 reduce-scatter.10
  1121.6 89.0 reduce-scatter.8
  1214.6 55.0 reduce-scatter.12
  1273.4 74.5 all-reduce.13
where the time goes:
time: 1370 us
  local copies, waits for them, and re-layouts  555 us (41%)
  waiting for transfers between devices  428 us (31%)
  matrix products  163 us (12%)
  blocking collectives  132 us (10%)
  other arithmetic  40.8 us (3%)
  loops' own time  29.1 us (2%)
  between operations  17.4 us (1%)
    while x84, local copies, waits for them, and re-layouts  216 us
    reshape x6, local copies, waits for them, and re-layouts, expand_diagonals(): flattened[:, :count_q * (span_len - 1)]  121 us
    unnamed x2, blocking collectives  96.1 us
    reduce_scatter x1, waiting for transfers between devices, per_device(): lax.psum_scatter(qkv_grad, ('fsdp', 'seq'), scatter_dimension=0, tiled=True)  92.1 us
    all_gather x1, waiting for transfers between devices, per_device(): lax.all_gather(expert_rows, ('fsdp', 'seq'), axis=0, tiled=True)  68.7 us
    all_gather x1, waiting for transfers between devices, per_device(): lax.all_gather(result_grad, ('fsdp', 'seq'), axis=0, tiled=True)  64.5 us
    slice x6, local copies, waits for them, and re-layouts, expand_diagonals(): flattened[:, :count_q * (span_len - 1)]  61.5 us
    unnamed x14, waiting for transfers between devices  59.2 us
  transfers between devices with their start and end apart: 13, of which 9 were waited for; matrix products, arithmetic and copies ran while one was open for 30% of the time, Pallas kernels for 0%

commit v1 on v0

v1 whole, which is shorter than its diff:
```python
import functools

import jax
import jax.numpy as jnp
from jax import lax
from jax.experimental import pallas as pl
from jax.experimental.pallas import tpu as pltpu
from jax.sharding import PartitionSpec as P

HEADS = 12
HEAD_DIM = 64
BUCKETS = 32
EXPERTS = 4
EPS = 1e-06
THRESHOLDS = (12, 16, 23, 32, 46, 64, 91)
SCORE_SCALE = 0.125
TILE = 128
BF = jnp.bfloat16
F32 = jnp.float32
VMEM_LIMIT = 48 * 1024 * 1024
GELU_A = 0.7978845608028654
GELU_B = 0.044715

VM = pl.BlockSpec(memory_space=pltpu.VMEM)
SM = pl.BlockSpec(memory_space=pltpu.SMEM)


def nn(a, b):
    return lax.dot_general(a, b, (((1,), (0,)), ((), ())), preferred_element_type=F32)


def nt(a, b):
    return lax.dot_general(a, b, (((1,), (1,)), ((), ())), preferred_element_type=F32)


def tn(a, b):
    return lax.dot_general(a, b, (((0,), (0,)), ((), ())), preferred_element_type=F32)


def bucket_of(distance):
    magnitude = jnp.abs(distance)
    far = jnp.full(distance.shape, 8, jnp.int32)
    for boundary in THRESHOLDS:
        far = far + (magnitude >= boundary).astype(jnp.int32)
    near = jnp.where(magnitude < 8, magnitude, far)
    return near + 16 * (distance > 0).astype(jnp.int32)


def band_buckets():
    row = lax.broadcasted_iota(jnp.int32, (TILE, 3 * TILE), 0)
    col = lax.broadcasted_iota(jnp.int32, (TILE, 3 * TILE), 1)
    return bucket_of(col - TILE - row)


def call(body, out_shape, in_specs, scratch=(), name=None, cost=None):
    return pl.pallas_call(
        body,
        out_shape=out_shape,
        in_specs=in_specs,
        out_specs=jax.tree.map(lambda _: VM, out_shape),
        scratch_shapes=list(scratch),
        compiler_params=pltpu.CompilerParams(vmem_limit_bytes=VMEM_LIMIT),
        name=name,
        cost_estimate=cost,
    )


def sds(shape, dtype):
    return jax.ShapeDtypeStruct(shape, dtype)


def band_kernel(heads, tab_ref, out_ref):
    buckets = band_buckets()
    for h in range(heads):
        out_ref[h] = jnp.zeros((TILE, 3 * TILE), F32)

    def step(b, carry):
        hit = buckets == b
        for h in range(heads):
            out_ref[h] = jnp.where(hit, tab_ref[b, h], out_ref[h])
        return carry

    lax.fori_loop(0, BUCKETS, step, 0)


def tile_scores(q, k, band_ref, tab_ref, h, qi, tiles):
    raw = nt(q, k)
    lo, hi = TILE * max(0, qi - 1), TILE * min(tiles, qi + 2)
    off = TILE - (TILE * qi - lo)
    parts = []
    if lo > 0:
        parts.append(raw[:, :lo] + tab_ref[BUCKETS // 2 - 1, h])
    parts.append(raw[:, lo:hi] + band_ref[h, :, off : off + hi - lo])
    if hi < TILE * tiles:
        parts.append(raw[:, hi:] + tab_ref[BUCKETS - 1, h])
    return jnp.concatenate(parts, axis=1) if len(parts) > 1 else parts[0]


def attend_kernel(n, heads, *refs):
    me_ref, tab_ref = refs[:2]
    xs = refs[2 : 2 + n]
    gain_ref, w_ref, band_ref = refs[2 + n : 5 + n]
    n1_ref, qkv_ref, lse_ref = refs[5 + n : 8 + n]
    outs = refs[8 + n : 8 + 2 * n]
    a_scr = refs[8 + 2 * n]
    me = me_ref[0]
    rows = xs[0].shape[0]
    tiles = n * rows // TILE
    width = 3 * heads * HEAD_DIM
    for k in range(n):
        start = pl.multiple_of(lax.rem(me + n - k, n) * rows, rows)
        x = xs[k][...].astype(F32)
        scale = lax.rsqrt(jnp.mean(x * x, axis=-1, keepdims=True) + EPS)
        normed = (x * scale * gain_ref[...]).astype(BF)
        n1_ref[pl.ds(start, rows), :] = normed
        qkv = nn(normed, w_ref[...])[:, :width].astype(BF)
        for c in range(3 * heads):
            qkv_ref[c, pl.ds(start, rows), :] = qkv[:, HEAD_DIM * c : HEAD_DIM * (c + 1)]

    def head(h, carry):
        keys = qkv_ref[heads + h]
        values = qkv_ref[2 * heads + h]
        for qi in range(tiles):
            at = slice(TILE * qi, TILE * (qi + 1))
            q = qkv_ref[h, at, :] * jnp.asarray(SCORE_SCALE, BF)
            s = tile_scores(q, keys, band_ref, tab_ref, h, qi, tiles)
            top = jnp.max(s, axis=-1, keepdims=True)
            raised = jnp.exp(s - top)
            total = jnp.sum(raised, axis=-1, keepdims=True)
            weights = (raised * (1.0 / total)).astype(BF)
            a_scr[h, at, :] = nn(weights, values)
            lse_ref[h, at, :] = top + jnp.log(total)
        return carry

    lax.fori_loop(0, heads, head, 0)
    for k in range(n):
        start = pl.multiple_of(lax.rem(me + k, n) * rows, rows)
        outs[k][...] = jnp.concatenate(
            [a_scr[h, pl.ds(start, rows), :] for h in range(heads)], axis=1
        ).astype(BF)


def before_kernel(n, cap, share, *refs):
    me_ref, x_ref, g_ref = refs[:3]
    a_refs = refs[3 : 3 + n]
    wo_ref, gain_ref, router_ref, idc_ref, idr_ref = refs[3 + n : 8 + n]
    y1_ref, probs_ref, target_ref = refs[8 + n : 11 + n]
    outs = refs[11 + n : 11 + 2 * n]
    me = me_ref[0]
    rows = x_ref.shape[0]
    hd = a_refs[0].shape[1]
    y1 = x_ref[...].astype(F32)
    for k in range(n):
        start = pl.multiple_of(lax.rem(me + n - k, n) * hd, hd)
        y1 = y1 + nn(a_refs[k][...], wo_ref[pl.ds(start, hd), :])
    y1_ref[...] = y1
    scale = lax.rsqrt(jnp.mean(y1 * y1, axis=-1, keepdims=True) + EPS)
    n2 = (y1 * scale * gain_ref[...]).astype(BF)
    lane = lax.broadcasted_iota(jnp.int32, (rows, TILE), 1)
    logits = jnp.where(lane < EXPERTS, nn(n2, router_ref[...]), -1e30)
    raised = jnp.exp(logits - jnp.max(logits, axis=-1, keepdims=True))
    raised = jnp.where(lane < EXPERTS, raised, 0.0)
    probs = raised / jnp.sum(raised, axis=-1, keepdims=True)
    probs_ref[...] = probs
    hot = lane == idc_ref[...]
    gating = jnp.sum(jnp.where(hot, probs, 0.0), axis=-1, keepdims=True)
    hot = hot.astype(F32)
    r0 = lax.broadcasted_iota(jnp.int32, (rows, rows), 0)
    r1 = lax.broadcasted_iota(jnp.int32, (rows, rows), 1)
    earlier = nn((r1 < r0).astype(BF), hot.astype(BF))
    slot = jnp.sum(earlier * hot, axis=-1, keepdims=True)
    target_ref[...] = idc_ref[...].astype(F32) * cap + slot
    hot_t = (lax.broadcasted_iota(jnp.int32, (16, rows), 0) == idr_ref[...]).astype(F32)
    earlier_t = nn(hot_t.astype(BF), (r0 < r1).astype(BF))
    slot_t = jnp.sum(earlier_t * hot_t, axis=0, keepdims=True)
    target_t = idr_ref[...].astype(F32) * cap + slot_t
    slot_grad = (gating * g_ref[...].astype(F32)).astype(BF)
    place = lax.broadcasted_iota(jnp.int32, (cap, rows), 0)
    for k in range(n):
        first = lax.div(lax.rem(me + k, n), share) * cap
        pick = (target_t == (first + place).astype(F32)).astype(BF)
        outs[k][0] = nn(pick, n2).astype(BF)
        outs[k][1] = nn(pick, slot_grad).astype(BF)


def gelu_parts(z):
    square = z * z
    t = jnp.tanh(GELU_A * (z + GELU_B * square * z))
    half = 0.5 * (1.0 + t)
    slope = half + 0.5 * z * (1.0 - t * t) * (GELU_A * (1.0 + 3.0 * GELU_B * square))
    return z * half, slope


def expert_kernel(f, n, block, rows_ref, *refs):
    w_refs = refs[:f]
    outs = refs[f : f + n]
    eo, dx = refs[f + n :]
    cap = outs[0].shape[1]
    eo[...] = jnp.zeros_like(eo)
    dx[...] = jnp.zeros_like(dx)
    for w in w_refs:

        def step(j, carry, w=w):
            at = pl.ds(pl.multiple_of(j * block, block), block)
            w_in, w_out = w[0, at, :], w[1, at, :]
            act, slope = gelu_parts(nt(rows_ref[0], w_in))
            back = (nt(rows_ref[1], w_out) * slope).astype(BF)
            eo[...] += nn(act.astype(BF), w_out)
            dx[...] += nn(back, w_in)
            return carry

        lax.fori_loop(0, w.shape[1] // block, step, 0)
    for k in range(n):
        outs[k][0] = eo[cap * k : cap * (k + 1), :].astype(BF)
        outs[k][1] = dx[cap * k : cap * (k + 1), :].astype(BF)


def expert_grad_kernel(f, block, *refs):
    row_refs = refs[:f]
    w_ref, out_ref, xin, deo = refs[f:]
    count = row_refs[0].shape[1]
    for i in range(f):
        xin[count * i : count * (i + 1), :] = row_refs[i][0]
        deo[count * i : count * (i + 1), :] = row_refs[i][1]

    def step(j, carry):
        at = pl.ds(pl.multiple_of(j * block, block), block)
        act, slope = gelu_parts(nt(w_ref[0, at, :], xin[...]))
        back = (nt(w_ref[1, at, :], deo[...]) * slope).astype(BF)
        out_ref[0, at, :] = nn(back, xin[...]).astype(BF)
        out_ref[1, at, :] = nn(act.astype(BF), deo[...]).astype(BF)
        return carry

    lax.fori_loop(0, w_ref.shape[1] // block, step, 0)


def after_kernel(n, cap, share, *refs):
    me_ref, g_ref, y1_ref, probs_ref, target_ref, idc_ref = refs[:6]
    back_refs = refs[6 : 6 + n]
    a_refs = refs[6 + n : 6 + 2 * n]
    wo_ref, gain_ref, router_ref = refs[6 + 2 * n : 9 + 2 * n]
    out_ref, dy1_ref, gwo_ref, small_ref = refs[9 + 2 * n : 13 + 2 * n]
    outs = refs[13 + 2 * n :]
    me = me_ref[0]
    rows = g_ref.shape[0]
    hd = a_refs[0].shape[1]
    y1 = y1_ref[...]
    g = g_ref[...].astype(F32)
    scale = lax.rsqrt(jnp.mean(y1 * y1, axis=-1, keepdims=True) + EPS)
    unit = y1 * scale
    n2 = (unit * gain_ref[...]).astype(BF)
    lane = lax.broadcasted_iota(jnp.int32, (rows, TILE), 1)
    hot = (lane == idc_ref[...]).astype(F32)
    probs = probs_ref[...]
    gating = jnp.sum(probs * hot, axis=-1, keepdims=True)
    place = lax.broadcasted_iota(jnp.int32, (rows, cap), 1)
    combined = jnp.zeros((rows, y1.shape[1]), F32)
    dn2 = jnp.zeros((rows, y1.shape[1]), F32)
    for k in range(n):
        first = lax.div(lax.rem(me + k, n), share) * cap
        pick = (target_ref[...] == (first + place).astype(F32)).astype(BF)
        combined = combined + nn(pick, back_refs[k][0])
        dn2 = dn2 + nn(pick, back_refs[k][1])
    out_ref[...] = (y1 + gating * combined).astype(BF)
    gate_grad = jnp.sum(g * combined, axis=-1, keepdims=True)
    dlogits = (gating * gate_grad) * (hot - probs)
    for e in range(EXPERTS):
        dn2 = dn2 + dlogits[:, e : e + 1] * router_ref[e : e + 1, :]
    high = dlogits.astype(BF)
    low = (dlogits - high.astype(F32)).astype(BF)
    router_grad = tn(high, n2) + tn(low, n2)
    small_ref[0:8, :] = router_grad[0:8, :]
    small_ref[8:16, :] = jnp.broadcast_to(
        jnp.sum(dn2 * unit, axis=0, keepdims=True), (8, y1.shape[1])
    )
    scaled = dn2 * gain_ref[...]
    inner = jnp.mean(scaled * unit, axis=-1, keepdims=True)
    dy1 = g + scale * (scaled - unit * inner)
    dy1_ref[...] = dy1
    db = dy1.astype(BF)
    for k in range(n):
        start = pl.multiple_of(lax.rem(me + k, n) * hd, hd)
        outs[k][...] = nt(db, wo_ref[pl.ds(start, hd), :]).astype(BF)
    for k in range(n):
        start = pl.multiple_of(lax.rem(me + n - k, n) * hd, hd)
        gwo_ref[pl.ds(start, hd), :] = tn(a_refs[k][...], db)


def attend_back_kernel(n, heads, *refs):
    me_ref, tab_ref = refs[:2]
    das = refs[2 : 2 + n]
    qkv_ref, lse_ref, band_ref = refs[2 + n : 5 + n]
    full_ref, bias_ref = refs[5 + n : 7 + n]
    outs = refs[7 + n : 7 + 2 * n]
    da_scr, grads, key_t, value_t, acc, left, right = refs[7 + 2 * n :]
    me = me_ref[0]
    rows = das[0].shape[0]
    tiles = n * rows // TILE
    buckets = band_buckets()
    for k in range(n):
        start = pl.multiple_of(lax.rem(me + n - k, n) * rows, rows)
        for h in range(heads):
            da_scr[h, pl.ds(start, rows), :] = das[k][:, HEAD_DIM * h : HEAD_DIM * (h + 1)]

    def head(h, carry):
        keys = qkv_ref[heads + h]
        values = qkv_ref[2 * heads + h]
        key_t[...] = jnp.zeros_like(key_t)
        value_t[...] = jnp.zeros_like(value_t)
        acc[...] = jnp.zeros_like(acc)
        left[...] = jnp.zeros_like(left)
        right[...] = jnp.zeros_like(right)
        for qi in range(tiles):
            at = slice(TILE * qi, TILE * (qi + 1))
            q = qkv_ref[h, at, :] * jnp.asarray(SCORE_SCALE, BF)
            da = da_scr[h, at, :]
            s = tile_scores(q, keys, band_ref, tab_ref, h, qi, tiles)
            p = jnp.exp(s - lse_ref[h, at, :])
            dp = nt(da, values)
            dot = jnp.sum(p * dp, axis=-1, keepdims=True)
            ds = p * (dp - dot)
            low = ds.astype(BF)
            grads[h, at, :] = nn(low, keys) * SCORE_SCALE
            key_t[...] += tn(q, low)
            value_t[...] += tn(da, p.astype(BF))
            lo, hi = max(0, qi - 1), min(tiles, qi + 2)
            off = TILE - TILE * (qi - lo)
            acc[:, off : off + TILE * (hi - lo)] += ds[:, TILE * lo : TILE * hi]
            if lo > 0:
                left[...] += sum(ds[:, TILE * b : TILE * (b + 1)] for b in range(lo))
            if hi < tiles:
                right[...] += sum(ds[:, TILE * b : TILE * (b + 1)] for b in range(hi, tiles))
        grads[heads + h] = key_t[...].T
        grads[2 * heads + h] = value_t[...].T
        for b in range(BUCKETS):
            line = jnp.sum(jnp.where(buckets == b, acc[...], 0.0), axis=0, keepdims=True)
            line = line[:, :TILE] + line[:, TILE : 2 * TILE] + line[:, 2 * TILE :]
            if b == BUCKETS // 2 - 1:
                line = line + jnp.sum(left[...], axis=0, keepdims=True)
            if b == BUCKETS - 1:
                line = line + jnp.sum(right[...], axis=0, keepdims=True)
            bias_ref[h, b : b + 1, :] = line
        return carry

    lax.fori_loop(0, heads, head, 0)
    for k in range(n):
        start = pl.multiple_of(lax.rem(me + k, n) * rows, rows)
        piece = jnp.concatenate(
            [grads[c, pl.ds(start, rows), :] for c in range(3 * heads)], axis=1
        ).astype(BF)
        outs[k][...] = piece
        full_ref[pl.ds(start, rows), :] = piece


def input_kernel(n, *refs):
    me_ref, x_ref, dy1_ref = refs[:3]
    ds = refs[3 : 3 + n]
    w_ref, gain_ref, out_ref = refs[3 + n :]
    me = me_ref[0]
    x = x_ref[...].astype(F32)
    scale = lax.rsqrt(jnp.mean(x * x, axis=-1, keepdims=True) + EPS)
    unit = x * scale
    dn1 = jnp.zeros(x.shape, F32)
    for k in range(n):
        dn1 = dn1 + nt(ds[k][...], w_ref[lax.rem(me + n - k, n)])
    scaled = dn1 * gain_ref[...]
    inner = jnp.mean(scaled * unit, axis=-1, keepdims=True)
    out_ref[...] = (dy1_ref[...] + scale * (scaled - unit * inner)).astype(BF)


def shift(value, n, k, axis="seq"):
    if k % n == 0:
        return value
    return lax.ppermute(value, axis, [(i, (i + k) % n) for i in range(n)])


def swap(value, n, bit, axis):
    return lax.ppermute(value, axis, [(i, i ^ bit) for i in range(n)])


def ahead_to_order(pieces, me):
    n = len(pieces)
    both = jnp.stack(pieces + pieces)
    return lax.dynamic_slice_in_dim(both, lax.rem(n - me, n), n, 0)


def behind_to_order(pieces, me):
    n = len(pieces)
    both = jnp.stack(pieces[::-1] + pieces[::-1])
    return lax.dynamic_slice_in_dim(both, n - 1 - me, n, 0)


def bits_of(n):
    return [1 << b for b in range(n.bit_length() - 1)]


def gather_swap(value, n, axis):
    pieces = [value]
    order = [0]
    for bit in reversed(bits_of(n)):
        pieces = pieces + [swap(p, n, bit, axis) for p in pieces]
        order = order + [m | bit for m in order]
    return [pieces[order.index(m)] for m in range(n)]


def swap_to_order(pieces, own):
    stacked = jnp.stack(pieces)
    return jnp.stack(
        [
            lax.dynamic_index_in_dim(stacked, jnp.bitwise_xor(i, own), 0, keepdims=False)
            for i in range(len(pieces))
        ]
    )


def scatter_swap(value, n, own, axis):
    for bit in bits_of(n):
        side = lax.rem(lax.div(own, bit), 2)
        paired = value.reshape((value.shape[0] // 2, 2) + value.shape[1:])
        keep = lax.dynamic_index_in_dim(paired, side, 1, keepdims=False)
        send = lax.dynamic_index_in_dim(paired, 1 - side, 1, keepdims=False)
        value = keep + swap(send.astype(BF), n, bit, axis).astype(F32)
    return value[0]


def scatter_seq(value, n, me):
    total = lax.dynamic_index_in_dim(value, me, 0, keepdims=False)
    for k in range(1, n):
        block = lax.dynamic_index_in_dim(value, lax.rem(me + k, n), 0, keepdims=False)
        total = total + shift(block.astype(BF), n, k).astype(F32)
    return total


def over_replica(value, n):
    low = value.astype(BF)
    if n == 1:
        return value
    if n == 2:
        return low.astype(F32) + swap(low, 2, 1, "replica").astype(F32)
    return lax.psum(low, "replica").astype(F32)


def per_device(
    tokens,
    cotangent,
    expert_ids,
    attn_gain,
    qkv_weight,
    output_weight,
    bias_table,
    ffn_gain,
    router_weight,
    expert_in,
    expert_out,
):
    _, rows, width = tokens.shape
    n, f, copies = lax.axis_size("seq"), lax.axis_size("fsdp"), lax.axis_size("replica")
    me, mine = lax.axis_index("seq"), lax.axis_index("fsdp")
    length = n * rows
    heads = -(-HEADS // n)
    hd = heads * HEAD_DIM
    total_hd = n * hd
    share = n // EXPERTS
    slots = rows * 5 // (4 * EXPERTS)
    cap = -(-slots // 16) * 16
    shard = qkv_weight.shape[0]
    unit_count = expert_in.shape[0]
    part = unit_count // share
    quarter = n * part
    block = 256 if quarter % 256 == 0 else quarter
    packed_width = -(-(3 * hd + 7) // TILE) * TILE
    me_arr = me.reshape(1)
    x = tokens[0]
    g = cotangent[0]
    ids = expert_ids[0]
    others = range(1, n)

    xs = [x] + [shift(x, n, k) for k in others]

    by_head = jnp.pad(qkv_weight.reshape(shard, 3, width), ((0, 0), (0, 0), (0, total_hd - width)))
    by_head = by_head.reshape(shard, 3, n, hd).transpose(2, 0, 1, 3).reshape(n, shard, 3 * hd)
    table_part = bias_table.shape[0]
    small = jnp.concatenate(
        [
            attn_gain[:, None],
            ffn_gain[:, None],
            router_weight,
            jnp.pad(bias_table, (0, shard - table_part))[:, None],
            jnp.zeros((shard, packed_width - 3 * hd - 7), BF),
        ],
        axis=1,
    )
    packed = jnp.concatenate(
        [by_head, jnp.broadcast_to(small[None], (n,) + small.shape)], axis=2
    )
    chunks = [
        shift(lax.dynamic_index_in_dim(packed, lax.rem(me + k, n), 0, keepdims=False), n, k)
        for k in range(n)
    ]
    chunk_rows = behind_to_order(chunks, me).reshape(n * shard, packed_width)
    own_w = swap_to_order(gather_swap(chunk_rows, f, "fsdp"), mine).reshape(width, packed_width)
    tail = own_w[:, 3 * hd : 3 * hd + 7]
    gain_one = tail[:, 0].astype(F32).reshape(1, width)
    gain_two = tail[:, 1].astype(F32).reshape(1, width)
    router = tail[:, 2 : 2 + EXPERTS]
    router_lanes = jnp.pad(router, ((0, 0), (0, TILE - EXPERTS)))
    router_rows = jnp.pad(router.astype(F32).T, ((0, 8 - EXPERTS), (0, 0)))
    table = tail[:, 6].reshape(f * n, shard)[:, :table_part].reshape(BUCKETS, HEADS).astype(F32)
    table = lax.dynamic_slice_in_dim(
        jnp.pad(table, ((0, 0), (0, n * heads - HEADS))), me * heads, heads, 1
    )
    band = call(
        functools.partial(band_kernel, heads),
        sds((heads, TILE, 3 * TILE), F32),
        [SM],
        name="bias_band",
    )(table)

    def expert_chunk(weight, k):
        dst = lax.rem(me + k, n)
        cut = lax.dynamic_slice(
            weight.reshape(share, part, EXPERTS, width),
            (lax.rem(dst, share), 0, lax.div(dst, share), 0),
            (1, part, 1, width),
        )
        return cut.reshape(part, width)

    pieces = [
        shift(jnp.stack([expert_chunk(expert_in, k), expert_chunk(expert_out, k)]), n, k)
        for k in range(n)
    ]
    own_expert = jnp.concatenate(pieces, axis=1)
    expert_parts = gather_swap(own_expert, f, "fsdp")

    wo = lax.all_gather(output_weight, ("fsdp", "seq"), axis=0, tiled=True)
    wo = jnp.pad(wo, ((0, total_hd - width), (0, 0)))
    wq = lax.all_gather(qkv_weight, ("fsdp", "seq"), axis=0, tiled=True)
    wq = jnp.pad(wq.reshape(width, 3, width), ((0, 0), (0, 0), (0, total_hd - width)))
    wq = wq.reshape(width, 3, n, hd).transpose(2, 0, 1, 3).reshape(n, width, 3 * hd)

    attended = call(
        functools.partial(attend_kernel, n, heads),
        [
            sds((length, width), BF),
            sds((3 * heads, length, HEAD_DIM), BF),
            sds((heads, length, 1), F32),
        ]
        + [sds((rows, hd), BF)] * n,
        [SM, SM] + [VM] * (n + 3),
        [pltpu.VMEM((heads, length, HEAD_DIM), F32)],
        name="attend",
    )(me_arr, table, *xs, gain_one, own_w, band)
    n1, qkv, lse = attended[:3]
    mixed = [shift(attended[3 + k], n, k) for k in range(n)]

    before = call(
        functools.partial(before_kernel, n, cap, share),
        [sds((rows, width), F32), sds((rows, TILE), F32), sds((rows, 1), F32)]
        + [sds((2, cap, width), BF)] * n,
        [SM] + [VM] * (n + 7),
        name="before_experts",
    )(me_arr, x, g, *mixed, wo, gain_two, router_lanes, ids, ids.reshape(1, rows))
    y1, probs, target = before[:3]
    arrived = [shift(before[3 + k], n, k) for k in range(n)]
    expert_rows = jnp.concatenate(arrived, axis=1)

    results = call(
        functools.partial(expert_kernel, f, n, block),
        [sds((2, cap, width), BF)] * n,
        [VM] * (f + 1),
        [pltpu.VMEM((n * cap, width), F32)] * 2,
        name="experts",
    )(expert_rows, *expert_parts)
    returned = [shift(results[k], n, n - k) for k in range(n)]

    all_rows = gather_swap(expert_rows, f, "fsdp")
    expert_grad = call(
        functools.partial(expert_grad_kernel, f, block),
        sds((2, quarter, width), BF),
        [VM] * (f + 1),
        [pltpu.VMEM((f * n * cap, width), BF)] * 2,
        name="expert_grads",
    )(*all_rows, own_expert)
    home = [
        shift(expert_grad[:, part * k : part * (k + 1), :], n, n - k) for k in range(n)
    ]
    home = [over_replica(piece, copies) for piece in home]
    home = ahead_to_order(home, me).reshape(EXPERTS, share, 2, part, width)
    home = home.transpose(2, 1, 3, 0, 4).reshape(2, unit_count, EXPERTS, width)

    after = call(
        functools.partial(after_kernel, n, cap, share),
        [
            sds((rows, width), BF),
            sds((rows, width), F32),
            sds((total_hd, width), F32),
            sds((16, width), F32),
        ]
        + [sds((rows, hd), BF)] * n,
        [SM] + [VM] * (2 * n + 8),
        name="after_experts",
    )(me_arr, g, y1, probs, target, ids, *returned, *mixed, wo, gain_two, router_rows)
    layer_out, dy1, wo_grad, small_grad = after[:4]
    das = [shift(after[4 + k], n, k) for k in range(n)]

    back = call(
        functools.partial(attend_back_kernel, n, heads),
        [sds((length, 3 * hd), BF), sds((heads, BUCKETS, TILE), F32)]
        + [sds((rows, 3 * hd), BF)] * n,
        [SM, SM] + [VM] * (n + 3),
        [
            pltpu.VMEM((heads, length, HEAD_DIM), BF),
            pltpu.VMEM((3 * heads, length, HEAD_DIM), F32),
            pltpu.VMEM((HEAD_DIM, length), F32),
            pltpu.VMEM((HEAD_DIM, length), F32),
            pltpu.VMEM((TILE, 3 * TILE), F32),
            pltpu.VMEM((TILE, TILE), F32),
            pltpu.VMEM((TILE, TILE), F32),
        ],
        name="attend_back",
    )(me_arr, table, *das, qkv, lse, band)
    dqkv, bias_lines = back[:2]
    own_dqkv = [shift(back[2 + k], n, k) for k in range(n)]
    input_grad = call(
        functools.partial(input_kernel, n),
        sds((rows, width), BF),
        [SM] + [VM] * (n + 4),
        name="input_grad",
    )(me_arr, x, dy1, *own_dqkv, wq, gain_one)

    qkv_grad = jnp.einsum("td,te->de", n1, dqkv, preferred_element_type=F32)
    qkv_grad = scatter_swap(qkv_grad.reshape(f, n, shard, 3 * hd), f, mine, "fsdp").astype(BF)
    qkv_grad = over_replica(qkv_grad, copies).astype(BF)
    qkv_grad = [
        shift(lax.dynamic_index_in_dim(qkv_grad, lax.rem(me + k, n), 0, keepdims=False), n, k)
        for k in range(n)
    ]
    qkv_grad = behind_to_order(qkv_grad, me).reshape(n, shard, 3, hd).transpose(1, 2, 0, 3)
    qkv_grad = qkv_grad.reshape(shard, 3, total_hd)[:, :, :width].reshape(shard, 3 * width)
    qkv_grad = qkv_grad.astype(F32)
    gain_one_grad = jnp.sum(qkv_grad * qkv_weight.astype(F32), axis=1) / attn_gain.astype(F32)

    wo_grad = wo_grad[:width].reshape(f, n, shard, width)
    wo_grad = scatter_swap(wo_grad, f, mine, "fsdp")
    wo_grad = over_replica(scatter_seq(wo_grad, n, me), copies)

    bias_rows = jnp.sum(bias_lines, axis=-1).T
    bias_rows = lax.dynamic_update_slice_in_dim(
        jnp.zeros((BUCKETS, n * heads), F32), bias_rows, me * heads, 1
    )[:, :HEADS].reshape(-1)
    sums = jnp.concatenate(
        [
            small_grad[: EXPERTS + 0],
            small_grad[8:9],
            jnp.pad(bias_rows, (0, width - BUCKETS * HEADS))[None],
        ],
        axis=0,
    )
    for axis, size in (("fsdp", f), ("replica", copies), ("seq", n)):
        for bit in bits_of(size):
            sums = sums + swap(sums, size, bit, axis)
    owner = mine * n + me
    router_grad = lax.dynamic_slice_in_dim(sums[:EXPERTS].T, owner * shard, shard, 0)
    gain_two_grad = lax.dynamic_slice_in_dim(sums[EXPERTS], owner * shard, shard, 0)
    bias_grad = lax.dynamic_slice_in_dim(sums[EXPERTS + 1], owner * table_part, table_part, 0)

    return (
        layer_out[None],
        input_grad[None],
        gain_one_grad,
        qkv_grad,
        wo_grad,
        bias_grad,
        gain_two_grad,
        router_grad,
        home[0],
        home[1],
    )


def solution(mesh):
    rows = P(("replica", "fsdp"), "seq", None)
    one, two, three = P(("fsdp", "seq")), P(("fsdp", "seq"), None), P(("fsdp", "seq"), None, None)
    return jax.shard_map(
        per_device,
        mesh=mesh,
        in_specs=(rows, rows, rows, one, two, two, one, one, two, three, three),
        out_specs=(rows, rows, one, two, two, one, one, two, three, three),
        check_vma=False,
    )
```

time: 1370 us -> 502 us (0.37)
  local copies, waits for them, and re-layouts: 555 us -> 64.9 us
  waiting for transfers between devices: 428 us -> 223 us
  matrix products: 163 us -> 1.44 us
  blocking collectives: 132 us -> 0 us
  starting transfers between devices: 0.69 us -> 83.3 us
  Pallas kernels: 0 us -> 71.7 us
  loops' own time: 29.1 us -> 0 us
    ppermute x0 -> x57, waiting for transfers between devices: none -> 223 us  [the longest x33 168 us: shift(): return lax.ppermute(value, axis, [(i, (i + k) % n) for i in range(n)])]
    while x85 -> x0, local copies, waits for them, and re-layouts: 216 us -> none
    reduce_scatter x3 -> x0, waiting for transfers between devices: 187 us -> none  [the longest x1 92.1 us: per_device(): lax.psum_scatter(qkv_grad, ('fsdp', 'seq'), scatter_dimension=0, tiled=True)]
    all_gather x8 -> x2, waiting for transfers between devices: 175 us -> 0.01 us  [the longest x1 0.01 us: per_device(): wo = lax.all_gather(output_weight, ('fsdp', 'seq'), axis=0, tiled=True)]
    dot_general x40 -> x1, matrix products: 162 us -> 1.44 us  [per_device(): qkv_grad = jnp.einsum('td,te->de', n1, dqkv, preferred_element_type=F32)]
    reshape x11 -> x5, local copies, waits for them, and re-layouts: 154 us -> 7.72 us  [the longest x1 5.94 us: per_device(): wq.reshape(width, 3, n, hd).transpose(2, 0, 1, 3).reshape(n, width, 3 * hd)]
    slice x16 -> x7, local copies, waits for them, and re-layouts: 108 us -> 3.2 us  [the longest x1 2.84 us: per_device(): expert_grad[:, part * k:part * (k + 1), :]]
    unnamed x2 -> x0, blocking collectives: 96.1 us -> none
  transfers between devices with their start and end apart: 13 -> 59, of which waited for: 9 -> 25; matrix products, arithmetic and copies ran while one was open for 30% -> 17% of each run, Pallas kernels for 0% -> 14%
where the time goes in v1:
time: 502 us; the launch traced here: 493 us
  waiting for transfers between devices  223 us (44%)
  starting transfers between devices  83.3 us (17%)
  Pallas kernels  71.7 us (14%)
  local copies, waits for them, and re-layouts  64.9 us (13%)
  other arithmetic  32.6 us (6%)
  between operations  15.3 us (3%)
    ppermute x33, waiting for transfers between devices, shift(): return lax.ppermute(value, axis, [(i, (i + k) % n) for i in range(n)])  168 us
    ppermute x24, waiting for transfers between devices, swap(): return lax.ppermute(value, axis, [(i, i ^ bit) for i in range(n)])  55.5 us
    ppermute x33, starting transfers between devices, shift(): return lax.ppermute(value, axis, [(i, (i + k) % n) for i in range(n)])  54 us
    ppermute x24, starting transfers between devices, swap(): return lax.ppermute(value, axis, [(i, i ^ bit) for i in range(n)])  29.2 us
    unnamed x98, local copies, waits for them, and re-layouts  19.2 us
    pallas_call x1, Pallas kernels, per_device(): call(functools.partial(attend_back_kernel, n, heads), [sds((length, 3 * h...  18.1 us
    unnamed x8, other arithmetic  16.5 us
    pallas_call x1, Pallas kernels, per_device(): call(functools.partial(attend_kernel, n, heads), [sds((length, width), BF...  15.4 us
  transfers between devices with their start and end apart: 59, of which 25 were waited for; matrix products, arithmetic and copies ran while one was open for 17% of the time, Pallas kernels for 14%

profile of v1, /device:TPU:0, one launch (start us, length us, event | category | flops | bytes accessed | tf_op | source)
XLA Modules:
  0.0 492.6 jit_solution(11129420133702127726)
XLA Ops:
  13.1 5.0 %collective-permute-start = (bf16[48,640]{1,0:T(8,128)(2,1)}, bf16[48,640]{1,0:T(8,128)(2,1)S(1)}, u32[]{:S(2)}, u32[]{:S(2)}) collective-permute-start(bf16[48,640]{1,0:T(8,128)(2,1)} %get-tuple-element.138), channel_id=1, source_target_pairs={{0,3},{1,0},{2,1},{3,2},{4,7},{5,4},{6,5},{7,6},{8,11},{9,8},{10,9... | collective-permute-start | bytes 184328 | tf_op jit(solution)/shard_map/ppermute | solution.py:374
  19.2 6.2 %constant_dynamic-slice_fusion.9 = (bf16[192,1,768]{2,1,0:T(2,128)(2,1)}, bf16[192,1,768]{2,1,0:T(2,128)(2,1)S(1)}, bf16[192,1,768]{2,1,0:T(2,128)(2,1)S(1)}, bf...) fusion(bf16[192,4,768]{2,1,0:T(4,128)(2,1)S(1)} %copy-done.27, ...), kind=kLoop, calls=%fused_computation.107 | loop fusion | bytes 4718608 | tf_op jit(solution)/shard_map/dynamic-slice.1
  26.4 2.8 collective-permute-start.17
  36.6 2.4 collective-permute-done.4
  41.2 3.8 collective-permute-done.17
  44.9 4.2 collective-permute-start.8
  49.1 57.3 %collective-permute-done.16 = bf16[2,192,768]{2,1,0:T(8,128)(2,1)} collective-permute-done((bf16[2,192,768]{2,1,0:T(8,128)(2,1)}, bf16[2,192,768]{2,1,0:T(8,128)(2,1)}, u32[]{:S(2)}, u32[]{:S(2)}) %collective-permute-start.16) | collective-permute-done | bytes 589856 | tf_op jit(solution)/shard_map/ppermute | solution.py:374
  106.9 2.6 pad_maximum_fusion.refs_0_.refs_4_
  113.6 2.5 bias_band.1.refs_8_
  119.1 15.4 %attend.1 = (bf16[1024,768]{1,0:T(8,128)(2,1)S(1)}, bf16[9,1024,64]{2,1,0:T(8,128)(2,1)}, f32[3,1024,1]{2,1,0:T(8,128)}, bf16[256,192]{1,0:T(8,128)(2,1)S(1)}, b...) custom-call(s32[1]{0:T(128)} %bitcast.refs_0_, ...), custom_call_target="tpu_custom_call" | custom-call | tf_op jit(solution)/shard_map/attend/pallas_call | solution.py:541
  135.7 4.8 collective-permute-start.9
  140.5 2.5 collective-permute-start.10
  147.0 5.1 %collective-permute-done.10.refs_5_.refs_12_ = bf16[256,192]{1,0:T(8,128)(2,1)S(1)} collective-permute-done((bf16[256,192]{1,0:T(8,128)(2,1)}, bf16[256,192]{1,0:T(8,128)(2,1)S(1)}, u32[]{:S(2)}, u32[]{:S(2)}) %collective-permute-start.10) | collective-permute-done | bytes 98336 | tf_op jit(solution)/shard_map/ppermute | solution.py:374
  160.4 2.6 collective-permute-start.12
  165.4 5.8 %collective-permute-done.12 = bf16[2,80,768]{2,1,0:T(8,128)(2,1)S(1)} collective-permute-done((bf16[2,80,768]{2,1,0:T(8,128)(2,1)S(1)}, bf16[2,80,768]{2,1,0:T(8,128)(2,1)S(1)}, u32[]{:S(2)}, u32[]{:S(2)}) %collective-permute-start.12) | collective-permute-done | bytes 245792 | tf_op jit(solution)/shard_map/ppermute | solution.py:374
  171.2 9.5 %collective-permute-done.13 = bf16[2,80,768]{2,1,0:T(8,128)(2,1)S(1)} collective-permute-done((bf16[2,80,768]{2,1,0:T(8,128)(2,1)S(1)}, bf16[2,80,768]{2,1,0:T(8,128)(2,1)S(1)}, u32[]{:S(2)}, u32[]{:S(2)}) %collective-permute-start.13) | collective-permute-done | bytes 245792 | tf_op jit(solution)/shard_map/ppermute | solution.py:374
  182.8 21.5 %collective-permute-done.48.refs_2_ = bf16[2,320,768]{2,1,0:T(8,128)(2,1)S(1)} collective-permute-done((bf16[2,320,768]{2,1,0:T(8,128)(2,1)S(1)}, bf16[2,320,768]{2,1,0:T(8,128)(2,1)S(1)}, u32[]{:S(2)}, u32[]{:S(2)}) %collective-permute-start.48) | collective-permute-done | bytes 983072 | tf_op jit(solution)/shard_map/ppermute | solution.py:378
  204.4 2.6 collective-permute-done.49.refs_3_
  206.9 10.2 %expert_grads.1 = bf16[2,768,768]{2,1,0:T(8,128)(2,1)} custom-call(bf16[2,320,768]{2,1,0:T(8,128)(2,1)S(1)} %constant_dynamic-update-slice_fusion.2.rows_ref.refs_0_, bf16[2,320,768]{2,1,0:T(8,128)(2,1)S(1)} %collective-permute-done.47.refs_1_, bf16[2,320,768]{2,1,0:T(8,128)(2,1)S(1)} %collective-permute-done.48.refs_2_, ...), custom_call_target="tpu_custom_call" | custom-call | tf_op jit(solution)/shard_map/expert_grads/pallas_call | solution.py:577
  217.2 2.8 fusion.20
  220.0 6.4 %collective-permute-start.51 = (bf16[2,192,768]{2,1,0:T(8,128)(2,1)S(1)}, bf16[2,192,768]{2,1,0:T(8,128)(2,1)}, u32[]{:S(2)}, u32[]{:S(2)}) collective-permute-start(bf16[2,192,768]{2,1,0:T(8,128)(2,1)S(1)} %get-tuple-element.120), channel_id=1, source_target_pairs={{0,3},{1,0},{2,1},{3,2},{4,7},{5,4},{6,5},{7,6},{8,11},{9,8},{10,9... | collective-permute-start | bytes 1769480 | tf_op jit(solution)/shard_map/ppermute | solution.py:374
  228.8 11.4 %collective-permute-done.51 = bf16[2,192,768]{2,1,0:T(8,128)(2,1)} collective-permute-done((bf16[2,192,768]{2,1,0:T(8,128)(2,1)S(1)}, bf16[2,192,768]{2,1,0:T(8,128)(2,1)}, u32[]{:S(2)}, u32[]{:S(2)}) %collective-permute-start.51) | collective-permute-done | bytes 589856 | tf_op jit(solution)/shard_map/ppermute | solution.py:374
  244.2 37.1 %collective-permute-done.53 = bf16[2,192,768]{2,1,0:T(8,128)(2,1)} collective-permute-done((bf16[2,192,768]{2,1,0:T(8,128)(2,1)}, bf16[2,192,768]{2,1,0:T(8,128)(2,1)}, u32[]{:S(2)}, u32[]{:S(2)}) %collective-permute-start.53) | collective-permute-done | bytes 589856 | tf_op jit(solution)/shard_map/ppermute | solution.py:374
  282.8 15.0 %experts.1 = (bf16[2,80,768]{2,1,0:T(8,128)(2,1)S(1)}, bf16[2,80,768]{2,1,0:T(8,128)(2,1)S(1)}, bf16[2,80,768]{2,1,0:T(8,128)(2,1)S(1)}, bf16[2,80,768]{2,1,0:T(8,128)(2,1)S(1)}) custom-call(bf16[2,320,768]{2,1,0:T(8,128)(2,1)S(1)} %constant_dynamic-update-slice_fusion.2.rows_ref.refs_0_, bf16[2,768,768]{2,1,0:T(8,128)(2,1)} %pad_maximum_fusion.refs_0_.refs_4_, ...), custom_call_target="tpu_custom_call" | custom-call | tf_op jit(solution)/shard_map/experts/pallas_call | solution.py:567
  302.3 10.0 %collective-permute-done.21.refs_7_ = bf16[2,80,768]{2,1,0:T(8,128)(2,1)S(1)} collective-permute-done((bf16[2,80,768]{2,1,0:T(8,128)(2,1)S(1)}, bf16[2,80,768]{2,1,0:T(8,128)(2,1)S(1)}, u32[]{:S(2)}, u32[]{:S(2)}) %collective-permute-start.21) | collective-permute-done | bytes 245792 | tf_op jit(solution)/shard_map/ppermute | solution.py:374
  312.3 2.5 collective-permute-start.56
  314.8 15.4 %collective-permute-done.22.refs_8_ = bf16[2,80,768]{2,1,0:T(8,128)(2,1)S(1)} collective-permute-done((bf16[2,80,768]{2,1,0:T(8,128)(2,1)S(1)}, bf16[2,80,768]{2,1,0:T(8,128)(2,1)S(1)}, u32[]{:S(2)}, u32[]{:S(2)}) %collective-permute-start.22) | collective-permute-done | bytes 245792 | tf_op jit(solution)/shard_map/ppermute | solution.py:374
  330.2 4.1 after_experts.1
  337.7 3.1 collective-permute-start.26
  345.5 2.4 bitcast_dynamic-update-slice_fusion
  350.1 2.6 bitcast_dynamic-update-slice_fusion.5
  355.0 18.1 %attend_back.1 = (bf16[1024,576]{1,0:T(8,128)(2,1)S(1)}, f32[3,32,128]{2,1,0:T(8,128)S(1)}, bf16[256,576]{1,0:T(8,128)(2,1)S(1)}, bf16[256,576]{1,0:T(8,128)(2,1...) custom-call(s32[1]{0:T(128)} %bitcast.refs_0_, f32[32,3]{1,0:T(8,128)S(1)} %constant_dynamic-slice_fusion.11.tab_ref.refs_1_, ...), custom_call_target="tpu_custom_call" | custom-call | tf_op jit(solution)/shard_map/attend_back/pallas_call | solution.py:606
  379.6 2.6 dynamic-slice_bitcast_fusion
  384.1 2.9 copy.126
  387.0 2.9 copy.127
  390.8 3.8 collective-permute-start.45
  396.1 8.8 %collective-permute-done.45 = f32[6,768]{1,0:T(8,128)S(1)} collective-permute-done((f32[6,768]{1,0:T(8,128)S(1)}, f32[6,768]{1,0:T(8,128)S(1)}, u32[]{:S(2)}, u32[]{:S(2)}) %collective-permute-start.45) | collective-permute-done | bytes 18464 | tf_op jit(solution)/shard_map/ppermute | solution.py:378
  404.8 4.6 collective-permute-start.46
  409.6 5.8 %collective-permute-done.46 = f32[6,768]{1,0:T(8,128)S(1)} collective-permute-done((f32[6,768]{1,0:T(8,128)S(1)}, f32[6,768]{1,0:T(8,128)S(1)}, u32[]{:S(2)}, u32[]{:S(2)}) %collective-permute-start.46) | collective-permute-done | bytes 18464 | tf_op jit(solution)/shard_map/ppermute | solution.py:378
  420.7 7.7 %collective-permute-done.37 = bf16[1,4,48,768]{3,2,1,0:T(8,128)(2,1)S(1)} collective-permute-done((bf16[1,4,48,768]{3,2,1,0:T(8,128)(2,1)S(1)}, bf16[1,4,48,768]{3,2,1,0:T(8,128)(2,1)S(1)}, u32[]{:S(2)}, u32[]{:S(2)}) %collective-permute-start.37) | collective-permute-done | bytes 294944 | tf_op jit(solution)/shard_map/ppermute | solution.py:378
  429.1 2.5 collective-permute-done.31
  439.3 3.8 collective-permute-done.32
  443.8 5.1 %collective-permute-start.34 = (bf16[48,576]{1,0:T(8,128)(2,1)S(1)}, bf16[48,576]{1,0:T(8,128)(2,1)S(1)}, u32[]{:S(2)}, u32[]{:S(2)}) collective-permute-start(bf16[48,576]{1,0:T(8,128)(2,1)S(1)} %get-tuple-element.141), channel_id=1, source_target_pairs={{0,2},{1,3},{2,0},{3,1},{4,6},{5,7},{6,4},{7,5},{8,10},{9,11},{10,... | collective-permute-start | bytes 165896 | tf_op jit(solution)/shard_map/ppermute | solution.py:374
  451.7 3.9 collective-permute-done.35
  465.0 5.8 %copy.119 = bf16[768,2304]{0,1:T(8,128)(2,1)} copy(bf16[768,2304]{1,0:T(8,128)(2,1)} %all-gather.5.cloned.1.call-done) | data formatting | bytes 7077888 | tf_op jit(solution)/shard_map/all_gather | solution.py:537
  470.8 4.1 copy.120
  474.9 5.9 %copy.121.refs_7_ = bf16[4,768,576]{2,1,0:T(8,128)(2,1)} copy(bf16[4,768,576]{1,2,0:T(8,128)(2,1)} %bitcast.153) | data formatting | bytes 7077888 | tf_op jit(solution)/shard_map/reshape | solution.py:539
  480.8 4.4 input_grad.1
  (268 shorter events, 105.0 us)
Async XLA Ops:
  7.2 146.2 %all-gather.3.cloned.1.call-start = ((), (), s32[]{:S(2)}) async-start(), calls=%async_computation | async-start | bytes 1253376 | tf_op jit(solution)/shard_map/all_gather | solution.py:535
  13.1 19.2 %collective-permute-start = (bf16[48,640]{1,0:T(8,128)(2,1)}, bf16[48,640]{1,0:T(8,128)(2,1)S(1)}, u32[]{:S(2)}, u32[]{:S(2)}) collective-permute-start(bf16[48,640]{1,0:T(8,128)(2,1)} %get-tuple-element.138), channel_id=1, source_target_pairs={{0,3},{1,0},{2,1},{3,2},{4,7},{5,4},{6,5},{7,6},{8,11},{9,8},{10,9... | collective-permute-start | bytes 184328 | tf_op jit(solution)/shard_map/ppermute | solution.py:374
  18.1 14.2 %collective-permute-start.1 = (bf16[48,640]{1,0:T(8,128)(2,1)}, bf16[48,640]{1,0:T(8,128)(2,1)S(1)}, u32[]{:S(2)}, u32[]{:S(2)}) collective-permute-start(bf16[48,640]{1,0:T(8,128)(2,1)} %get-tuple-element.139), channel_id=1, source_target_pairs={{0,2},{1,3},{2,0},{3,1},{4,6},{5,7},{6,4},{7,5},{8,10},{9,11},{10,... | collective-permute-start | bytes 184328 | tf_op jit(solution)/shard_map/ppermute | solution.py:374
  18.1 14.2 %collective-permute-start.2 = (bf16[48,640]{1,0:T(8,128)(2,1)S(1)}, bf16[48,640]{1,0:T(8,128)(2,1)S(1)}, u32[]{:S(2)}, u32[]{:S(2)}) collective-permute-start(bf16[48,640]{1,0:T(8,128)(2,1)S(1)} %get-tuple-element.137), channel_id=1, source_target_pairs={{0,1},{1,2},{2,3},{3,0},{4,5},{5,6},{6,7},{7,4},{8,9},{9,10},{10,1... | collective-permute-start | bytes 184328 | tf_op jit(solution)/shard_map/ppermute | solution.py:374
  19.1 445.9 %all-gather.5.cloned.1.call-start = ((), (), s32[]{:S(2)}) async-start(), calls=%async_computation.1 | async-start | bytes 3760128 | tf_op jit(solution)/shard_map/all_gather | solution.py:537
  26.4 18.5 %collective-permute-start.17 = (bf16[2,192,768]{2,1,0:T(8,128)(2,1)}, bf16[2,192,768]{2,1,0:T(8,128)(2,1)S(1)}, u32[]{:S(2)}, u32[]{:S(2)}) collective-permute-start(bf16[2,192,768]{2,1,0:T(8,128)(2,1)} %pad_maximum_fusion.5), channel_id=1, source_target_pairs={{0,3},{1,0},{2,1},{3,2},{4,7},{5,4},{6,5},{7,6},{8,11},{9,8},{10,9... | collective-permute-start | bytes 1769480 | tf_op jit(solution)/shard_map/ppermute | solution.py:374
  30.2 76.2 %collective-permute-start.16 = (bf16[2,192,768]{2,1,0:T(8,128)(2,1)}, bf16[2,192,768]{2,1,0:T(8,128)(2,1)}, u32[]{:S(2)}, u32[]{:S(2)}) collective-permute-start(bf16[2,192,768]{2,1,0:T(8,128)(2,1)} %pad_maximum_fusion.4), channel_id=1, source_target_pairs={{0,2},{1,3},{2,0},{3,1},{4,6},{5,7},{6,4},{7,5},{8,10},{9,11},{10,... | collective-permute-start | bytes 1769480 | tf_op jit(solution)/shard_map/ppermute | solution.py:374
  32.3 74.1 %collective-permute-start.15 = (bf16[2,192,768]{2,1,0:T(8,128)(2,1)}, bf16[2,192,768]{2,1,0:T(8,128)(2,1)}, u32[]{:S(2)}, u32[]{:S(2)}) collective-permute-start(bf16[2,192,768]{2,1,0:T(8,128)(2,1)} %pad_maximum_fusion.3), channel_id=1, source_target_pairs={{0,1},{1,2},{2,3},{3,0},{4,5},{5,6},{6,7},{7,4},{8,9},{9,10},{10,1... | collective-permute-start | bytes 1769480 | tf_op jit(solution)/shard_map/ppermute | solution.py:374
  34.2 82.0 %collective-permute-start.6 = (bf16[256,768]{1,0:T(8,128)(2,1)S(1)}, bf16[256,768]{1,0:T(8,128)(2,1)S(1)}, u32[]{:S(2)}, u32[]{:S(2)}) collective-permute-start(bf16[256,768]{1,0:T(8,128)(2,1)S(1)} %bitcast.143), channel_id=1, source_target_pairs={{0,1},{1,2},{2,3},{3,0},{4,5},{5,6},{6,7},{7,4},{8,9},{9,10},{10,1... | collective-permute-start | bytes 1179656 | tf_op jit(solution)/shard_map/ppermute | solution.py:374
  39.1 77.1 %collective-permute-start.7 = (bf16[256,768]{1,0:T(8,128)(2,1)S(1)}, bf16[256,768]{1,0:T(8,128)(2,1)S(1)}, u32[]{:S(2)}, u32[]{:S(2)}) collective-permute-start(bf16[256,768]{1,0:T(8,128)(2,1)S(1)} %bitcast.144), channel_id=1, source_target_pairs={{0,2},{1,3},{2,0},{3,1},{4,6},{5,7},{6,4},{7,5},{8,10},{9,11},{10,... | collective-permute-start | bytes 1179656 | tf_op jit(solution)/shard_map/ppermute | solution.py:374
  44.9 72.4 %collective-permute-start.8 = (bf16[256,768]{1,0:T(8,128)(2,1)S(1)}, bf16[256,768]{1,0:T(8,128)(2,1)S(1)}, u32[]{:S(2)}, u32[]{:S(2)}) collective-permute-start(bf16[256,768]{1,0:T(8,128)(2,1)S(1)} %bitcast.145), channel_id=1, source_target_pairs={{0,3},{1,0},{2,1},{3,2},{4,7},{5,4},{6,5},{7,6},{8,11},{9,8},{10,9... | collective-permute-start | bytes 1179656 | tf_op jit(solution)/shard_map/ppermute | solution.py:374
  109.5 72.9 %collective-permute-start.19 = (bf16[2,768,768]{2,1,0:T(8,128)(2,1)}, bf16[2,768,768]{2,1,0:T(8,128)(2,1)}, u32[]{:S(2)}, u32[]{:S(2)}) collective-permute-start(bf16[2,768,768]{2,1,0:T(8,128)(2,1)} %pad_maximum_fusion.refs_0_.refs_4_), channel_id=1, source_target_pairs={{0,8},{4,12},{8,0},{12,4},{1,9},{5,13},{9,1},{13,5},{2,10},{6,14},... | collective-permute-start | bytes 7077896 | tf_op jit(solution)/shard_map/ppermute | solution.py:378
  135.7 11.4 %collective-permute-start.9 = (bf16[256,192]{1,0:T(8,128)(2,1)}, bf16[256,192]{1,0:T(8,128)(2,1)S(1)}, u32[]{:S(2)}, u32[]{:S(2)}) collective-permute-start(bf16[256,192]{1,0:T(8,128)(2,1)} %get-tuple-element.43), channel_id=1, source_target_pairs={{0,1},{1,2},{2,3},{3,0},{4,5},{5,6},{6,7},{7,4},{8,9},{9,10},{10,1... | collective-permute-start | bytes 294920 | tf_op jit(solution)/shard_map/ppermute | solution.py:374
  140.5 11.6 %collective-permute-start.10 = (bf16[256,192]{1,0:T(8,128)(2,1)}, bf16[256,192]{1,0:T(8,128)(2,1)S(1)}, u32[]{:S(2)}, u32[]{:S(2)}) collective-permute-start(bf16[256,192]{1,0:T(8,128)(2,1)} %get-tuple-element.44), channel_id=1, source_target_pairs={{0,2},{1,3},{2,0},{3,1},{4,6},{5,7},{6,4},{7,5},{8,10},{9,11},{10,... | collective-permute-start | bytes 294920 | tf_op jit(solution)/shard_map/ppermute | solution.py:374
  143.0 9.8 %collective-permute-start.11 = (bf16[256,192]{1,0:T(8,128)(2,1)S(1)}, bf16[256,192]{1,0:T(8,128)(2,1)S(1)}, u32[]{:S(2)}, u32[]{:S(2)}) collective-permute-start(bf16[256,192]{1,0:T(8,128)(2,1)S(1)} %get-tuple-element.45), channel_id=1, source_target_pairs={{0,3},{1,0},{2,1},{3,2},{4,7},{5,4},{6,5},{7,6},{8,11},{9,8},{10,9... | collective-permute-start | bytes 294920 | tf_op jit(solution)/shard_map/ppermute | solution.py:374
  160.4 10.8 %collective-permute-start.12 = (bf16[2,80,768]{2,1,0:T(8,128)(2,1)S(1)}, bf16[2,80,768]{2,1,0:T(8,128)(2,1)S(1)}, u32[]{:S(2)}, u32[]{:S(2)}) collective-permute-start(bf16[2,80,768]{2,1,0:T(8,128)(2,1)S(1)} %get-tuple-element.50), channel_id=1, source_target_pairs={{0,1},{1,2},{2,3},{3,0},{4,5},{5,6},{6,7},{7,4},{8,9},{9,10},{10,1... | collective-permute-start | bytes 737288 | tf_op jit(solution)/shard_map/ppermute | solution.py:374
  163.0 17.6 %collective-permute-start.13 = (bf16[2,80,768]{2,1,0:T(8,128)(2,1)S(1)}, bf16[2,80,768]{2,1,0:T(8,128)(2,1)S(1)}, u32[]{:S(2)}, u32[]{:S(2)}) collective-permute-start(bf16[2,80,768]{2,1,0:T(8,128)(2,1)S(1)} %get-tuple-element.51), channel_id=1, source_target_pairs={{0,2},{1,3},{2,0},{3,1},{4,6},{5,7},{6,4},{7,5},{8,10},{9,11},{10,... | collective-permute-start | bytes 737288 | tf_op jit(solution)/shard_map/ppermute | solution.py:374
  163.6 17.1 %collective-permute-start.14 = (bf16[2,80,768]{2,1,0:T(8,128)(2,1)S(1)}, bf16[2,80,768]{2,1,0:T(8,128)(2,1)S(1)}, u32[]{:S(2)}, u32[]{:S(2)}) collective-permute-start(bf16[2,80,768]{2,1,0:T(8,128)(2,1)S(1)} %get-tuple-element.52), channel_id=1, source_target_pairs={{0,3},{1,0},{2,1},{3,2},{4,7},{5,4},{6,5},{7,6},{8,11},{9,8},{10,9... | collective-permute-start | bytes 737288 | tf_op jit(solution)/shard_map/ppermute | solution.py:374
  180.7 23.6 %collective-permute-start.48 = (bf16[2,320,768]{2,1,0:T(8,128)(2,1)S(1)}, bf16[2,320,768]{2,1,0:T(8,128)(2,1)S(1)}, u32[]{:S(2)}, u32[]{:S(2)}) collective-permute-start(bf16[2,320,768]{2,1,0:T(8,128)(2,1)S(1)} %constant_dynamic-update-slice_fusion.2.rows_ref.refs_0_), channel_id=1, source_target_pairs={{0,8},{4,12},{8,0},{12,4},{1,9},{5,13},{9,1},{13,5},{2,10},{6,14},... | collective-permute-start | bytes 2949128 | tf_op jit(solution)/shard_map/ppermute | solution.py:378
  182.3 46.5 %collective-permute-start.18 = (bf16[2,768,768]{2,1,0:T(8,128)(2,1)}, bf16[2,768,768]{2,1,0:T(8,128)(2,1)}, u32[]{:S(2)}, u32[]{:S(2)}) collective-permute-start(bf16[2,768,768]{2,1,0:T(8,128)(2,1)} %pad_maximum_fusion.refs_0_.refs_4_), channel_id=1, source_target_pairs={{0,4},{4,0},{8,12},{12,8},{1,5},{5,1},{9,13},{13,9},{2,6},{6,2},{1... | collective-permute-start | bytes 7077896 | tf_op jit(solution)/shard_map/ppermute | solution.py:378
  182.3 100.5 %collective-permute-start.20 = (bf16[2,768,768]{2,1,0:T(8,128)(2,1)}, bf16[2,768,768]{2,1,0:T(8,128)(2,1)}, u32[]{:S(2)}, u32[]{:S(2)}) collective-permute-start(bf16[2,768,768]{2,1,0:T(8,128)(2,1)} %collective-permute-done.19.refs_2_), channel_id=1, source_target_pairs={{0,4},{4,0},{8,12},{12,8},{1,5},{5,1},{9,13},{13,9},{2,6},{6,2},{1... | collective-permute-start | bytes 7077896 | tf_op jit(solution)/shard_map/ppermute | solution.py:378
  182.8 21.5 %collective-permute-start.47 = (bf16[2,320,768]{2,1,0:T(8,128)(2,1)S(1)}, bf16[2,320,768]{2,1,0:T(8,128)(2,1)S(1)}, u32[]{:S(2)}, u32[]{:S(2)}) collective-permute-start(bf16[2,320,768]{2,1,0:T(8,128)(2,1)S(1)} %constant_dynamic-update-slice_fusion.2.rows_ref.refs_0_), channel_id=1, source_target_pairs={{0,4},{4,0},{8,12},{12,8},{1,5},{5,1},{9,13},{13,9},{2,6},{6,2},{1... | collective-permute-start | bytes 2949128 | tf_op jit(solution)/shard_map/ppermute | solution.py:378
  220.0 20.2 %collective-permute-start.51 = (bf16[2,192,768]{2,1,0:T(8,128)(2,1)S(1)}, bf16[2,192,768]{2,1,0:T(8,128)(2,1)}, u32[]{:S(2)}, u32[]{:S(2)}) collective-permute-start(bf16[2,192,768]{2,1,0:T(8,128)(2,1)S(1)} %get-tuple-element.120), channel_id=1, source_target_pairs={{0,3},{1,0},{2,1},{3,2},{4,7},{5,4},{6,5},{7,6},{8,11},{9,8},{10,9... | collective-permute-start | bytes 1769480 | tf_op jit(solution)/shard_map/ppermute | solution.py:374
  226.5 54.8 %collective-permute-start.53 = (bf16[2,192,768]{2,1,0:T(8,128)(2,1)}, bf16[2,192,768]{2,1,0:T(8,128)(2,1)}, u32[]{:S(2)}, u32[]{:S(2)}) collective-permute-start(bf16[2,192,768]{2,1,0:T(8,128)(2,1)} %get-tuple-element.119), channel_id=1, source_target_pairs={{0,2},{1,3},{2,0},{3,1},{4,6},{5,7},{6,4},{7,5},{8,10},{9,11},{10,... | collective-permute-start | bytes 1769480 | tf_op jit(solution)/shard_map/ppermute | solution.py:374
  227.3 70.7 %collective-permute-start.50 = (bf16[2,192,768]{2,1,0:T(8,128)(2,1)}, bf16[2,192,768]{2,1,0:T(8,128)(2,1)}, u32[]{:S(2)}, u32[]{:S(2)}) collective-permute-start(bf16[2,192,768]{2,1,0:T(8,128)(2,1)} %get-tuple-element.121), channel_id=1, source_target_pairs={{0,16},{16,0},{1,17},{17,1},{2,18},{18,2},{3,19},{19,3},{4,20},{20... | collective-permute-start | bytes 1769480 | tf_op jit(solution)/shard_map/ppermute | solution.py:378
  228.8 69.2 %collective-permute-start.55 = (bf16[2,192,768]{2,1,0:T(8,128)(2,1)}, bf16[2,192,768]{2,1,0:T(8,128)(2,1)}, u32[]{:S(2)}, u32[]{:S(2)}) collective-permute-start(bf16[2,192,768]{2,1,0:T(8,128)(2,1)} %get-tuple-element.118), channel_id=1, source_target_pairs={{0,1},{1,2},{2,3},{3,0},{4,5},{5,6},{6,7},{7,4},{8,9},{9,10},{10,1... | collective-permute-start | bytes 1769480 | tf_op jit(solution)/shard_map/ppermute | solution.py:374
  240.2 97.5 %collective-permute-start.52 = (bf16[2,192,768]{2,1,0:T(8,128)(2,1)}, bf16[2,192,768]{2,1,0:T(8,128)(2,1)}, u32[]{:S(2)}, u32[]{:S(2)}) collective-permute-start(bf16[2,192,768]{2,1,0:T(8,128)(2,1)} %collective-permute-done.51), channel_id=1, source_target_pairs={{0,16},{16,0},{1,17},{17,1},{2,18},{18,2},{3,19},{19,3},{4,20},{20... | collective-permute-start | bytes 1769480 | tf_op jit(solution)/shard_map/ppermute | solution.py:378
  281.3 62.0 %collective-permute-start.54 = (bf16[2,192,768]{2,1,0:T(8,128)(2,1)}, bf16[2,192,768]{2,1,0:T(8,128)(2,1)S(1)}, u32[]{:S(2)}, u32[]{:S(2)}) collective-permute-start(bf16[2,192,768]{2,1,0:T(8,128)(2,1)} %collective-permute-done.53), channel_id=1, source_target_pairs={{0,16},{16,0},{1,17},{17,1},{2,18},{18,2},{3,19},{19,3},{4,20},{20... | collective-permute-start | bytes 1769480 | tf_op jit(solution)/shard_map/ppermute | solution.py:378
  297.9 14.4 %collective-permute-start.21 = (bf16[2,80,768]{2,1,0:T(8,128)(2,1)S(1)}, bf16[2,80,768]{2,1,0:T(8,128)(2,1)S(1)}, u32[]{:S(2)}, u32[]{:S(2)}) collective-permute-start(bf16[2,80,768]{2,1,0:T(8,128)(2,1)S(1)} %get-tuple-element.54), channel_id=1, source_target_pairs={{0,3},{1,0},{2,1},{3,2},{4,7},{5,4},{6,5},{7,6},{8,11},{9,8},{10,9... | collective-permute-start | bytes 737288 | tf_op jit(solution)/shard_map/ppermute | solution.py:374
  298.0 32.2 %collective-permute-start.22 = (bf16[2,80,768]{2,1,0:T(8,128)(2,1)S(1)}, bf16[2,80,768]{2,1,0:T(8,128)(2,1)S(1)}, u32[]{:S(2)}, u32[]{:S(2)}) collective-permute-start(bf16[2,80,768]{2,1,0:T(8,128)(2,1)S(1)} %get-tuple-element.55), channel_id=1, source_target_pairs={{0,2},{1,3},{2,0},{3,1},{4,6},{5,7},{6,4},{7,5},{8,10},{9,11},{10,... | collective-permute-start | bytes 737288 | tf_op jit(solution)/shard_map/ppermute | solution.py:374
  298.1 32.1 %collective-permute-start.23 = (bf16[2,80,768]{2,1,0:T(8,128)(2,1)S(1)}, bf16[2,80,768]{2,1,0:T(8,128)(2,1)S(1)}, u32[]{:S(2)}, u32[]{:S(2)}) collective-permute-start(bf16[2,80,768]{2,1,0:T(8,128)(2,1)S(1)} %get-tuple-element.56), channel_id=1, source_target_pairs={{0,1},{1,2},{2,3},{3,0},{4,5},{5,6},{6,7},{7,4},{8,9},{9,10},{10,1... | collective-permute-start | bytes 737288 | tf_op jit(solution)/shard_map/ppermute | solution.py:374
  312.3 33.2 %collective-permute-start.56 = (bf16[2,192,768]{2,1,0:T(8,128)(2,1)}, bf16[2,192,768]{2,1,0:T(8,128)(2,1)S(1)}, u32[]{:S(2)}, u32[]{:S(2)}) collective-permute-start(bf16[2,192,768]{2,1,0:T(8,128)(2,1)} %collective-permute-done.55), channel_id=1, source_target_pairs={{0,16},{16,0},{1,17},{17,1},{2,18},{18,2},{3,19},{19,3},{4,20},{20... | collective-permute-start | bytes 1769480 | tf_op jit(solution)/shard_map/ppermute | solution.py:378
  334.3 20.8 %collective-permute-start.24 = (bf16[256,192]{1,0:T(8,128)(2,1)S(1)}, bf16[256,192]{1,0:T(8,128)(2,1)S(1)}, u32[]{:S(2)}, u32[]{:S(2)}) collective-permute-start(bf16[256,192]{1,0:T(8,128)(2,1)S(1)} %get-tuple-element.60), channel_id=1, source_target_pairs={{0,1},{1,2},{2,3},{3,0},{4,5},{5,6},{6,7},{7,4},{8,9},{9,10},{10,1... | collective-permute-start | bytes 294920 | tf_op jit(solution)/shard_map/ppermute | solution.py:374
  336.4 18.6 %collective-permute-start.25 = (bf16[256,192]{1,0:T(8,128)(2,1)S(1)}, bf16[256,192]{1,0:T(8,128)(2,1)S(1)}, u32[]{:S(2)}, u32[]{:S(2)}) collective-permute-start(bf16[256,192]{1,0:T(8,128)(2,1)S(1)} %get-tuple-element.61), channel_id=1, source_target_pairs={{0,2},{1,3},{2,0},{3,1},{4,6},{5,7},{6,4},{7,5},{8,10},{9,11},{10,... | collective-permute-start | bytes 294920 | tf_op jit(solution)/shard_map/ppermute | solution.py:374
  337.7 17.3 %collective-permute-start.26 = (bf16[256,192]{1,0:T(8,128)(2,1)S(1)}, bf16[256,192]{1,0:T(8,128)(2,1)S(1)}, u32[]{:S(2)}, u32[]{:S(2)}) collective-permute-start(bf16[256,192]{1,0:T(8,128)(2,1)S(1)} %get-tuple-element.62), channel_id=1, source_target_pairs={{0,3},{1,0},{2,1},{3,2},{4,7},{5,4},{6,5},{7,6},{8,11},{9,8},{10,9... | collective-permute-start | bytes 294920 | tf_op jit(solution)/shard_map/ppermute | solution.py:374
  343.2 74.0 %collective-permute-start.36 = (bf16[2,4,48,768]{3,2,1,0:T(8,128)(2,1)}, bf16[2,4,48,768]{3,2,1,0:T(8,128)(2,1)}, u32[]{:S(2)}, u32[]{:S(2)}) collective-permute-start(bf16[2,4,48,768]{3,2,1,0:T(8,128)(2,1)} %fusion), channel_id=1, source_target_pairs={{0,4},{4,0},{8,12},{12,8},{1,5},{5,1},{9,13},{13,9},{2,6},{6,2},{1... | collective-permute-start | bytes 1769480 | tf_op jit(solution)/shard_map/ppermute | solution.py:378
  382.2 8.6 %collective-permute-start.44 = (f32[6,768]{1,0:T(8,128)S(1)}, f32[6,768]{1,0:T(8,128)S(1)}, u32[]{:S(2)}, u32[]{:S(2)}) collective-permute-start(f32[6,768]{1,0:T(8,128)S(1)} %add.209), channel_id=1, source_target_pairs={{0,16},{16,0},{1,17},{17,1},{2,18},{18,2},{3,19},{19,3},{4,20},{20... | collective-permute-start | bytes 55304 | tf_op jit(solution)/shard_map/ppermute | solution.py:378
  389.9 90.9 %collective-permute-start.27 = (bf16[256,576]{1,0:T(8,128)(2,1)}, bf16[256,576]{1,0:T(8,128)(2,1)S(1)}, u32[]{:S(2)}, u32[]{:S(2)}) collective-permute-start(bf16[256,576]{1,0:T(8,128)(2,1)} %get-tuple-element.66), channel_id=1, source_target_pairs={{0,1},{1,2},{2,3},{3,0},{4,5},{5,6},{6,7},{7,4},{8,9},{9,10},{10,1... | collective-permute-start | bytes 884744 | tf_op jit(solution)/shard_map/ppermute | solution.py:374
  390.2 90.7 %collective-permute-start.28 = (bf16[256,576]{1,0:T(8,128)(2,1)S(1)}, bf16[256,576]{1,0:T(8,128)(2,1)S(1)}, u32[]{:S(2)}, u32[]{:S(2)}) collective-permute-start(bf16[256,576]{1,0:T(8,128)(2,1)S(1)} %get-tuple-element.67), channel_id=1, source_target_pairs={{0,2},{1,3},{2,0},{3,1},{4,6},{5,7},{6,4},{7,5},{8,10},{9,11},{10,... | collective-permute-start | bytes 884744 | tf_op jit(solution)/shard_map/ppermute | solution.py:374
  390.8 14.0 %collective-permute-start.45 = (f32[6,768]{1,0:T(8,128)S(1)}, f32[6,768]{1,0:T(8,128)S(1)}, u32[]{:S(2)}, u32[]{:S(2)}) collective-permute-start(f32[6,768]{1,0:T(8,128)S(1)} %add.210), channel_id=1, source_target_pairs={{0,1},{1,0},{2,3},{3,2},{4,5},{5,4},{6,7},{7,6},{8,9},{9,8},{10,11... | collective-permute-start | bytes 55304 | tf_op jit(solution)/shard_map/ppermute | solution.py:378
  404.8 10.5 %collective-permute-start.46 = (f32[6,768]{1,0:T(8,128)S(1)}, f32[6,768]{1,0:T(8,128)S(1)}, u32[]{:S(2)}, u32[]{:S(2)}) collective-permute-start(f32[6,768]{1,0:T(8,128)S(1)} %add.211), channel_id=1, source_target_pairs={{0,2},{1,3},{2,0},{3,1},{4,6},{5,7},{6,4},{7,5},{8,10},{9,11},{10,... | collective-permute-start | bytes 55304 | tf_op jit(solution)/shard_map/ppermute | solution.py:378
  409.5 9.6 %collective-permute-start.30 = (bf16[2,4,48,576]{3,2,1,0:T(8,128)(2,1)S(1)}, bf16[2,4,48,576]{3,2,1,0:T(8,128)(2,1)S(1)}, u32[]{:S(2)}, u32[]{:S(2)}) collective-permute-start(bf16[2,4,48,576]{3,2,1,0:T(8,128)(2,1)S(1)} %fusion.1), channel_id=1, source_target_pairs={{0,4},{4,0},{8,12},{12,8},{1,5},{5,1},{9,13},{13,9},{2,6},{6,2},{1... | collective-permute-start | bytes 1327112 | tf_op jit(solution)/shard_map/ppermute | solution.py:378
  418.4 10.0 %collective-permute-start.37 = (bf16[1,4,48,768]{3,2,1,0:T(8,128)(2,1)S(1)}, bf16[1,4,48,768]{3,2,1,0:T(8,128)(2,1)S(1)}, u32[]{:S(2)}, u32[]{:S(2)}) collective-permute-start(bf16[1,4,48,768]{3,2,1,0:T(8,128)(2,1)S(1)} %dynamic-slice_convert_fusion.1), channel_id=1, source_target_pairs={{0,8},{4,12},{8,0},{12,4},{1,9},{5,13},{9,1},{13,5},{2,10},{6,14},... | collective-permute-start | bytes 884744 | tf_op jit(solution)/shard_map/ppermute | solution.py:378
  419.2 12.4 %collective-permute-start.31 = (bf16[1,4,48,576]{3,2,1,0:T(8,128)(2,1)S(1)}, bf16[1,4,48,576]{3,2,1,0:T(8,128)(2,1)S(1)}, u32[]{:S(2)}, u32[]{:S(2)}) collective-permute-start(bf16[1,4,48,576]{3,2,1,0:T(8,128)(2,1)S(1)} %dynamic-slice_convert_fusion.2), channel_id=1, source_target_pairs={{0,8},{4,12},{8,0},{12,4},{1,9},{5,13},{9,1},{13,5},{2,10},{6,14},... | collective-permute-start | bytes 663560 | tf_op jit(solution)/shard_map/ppermute | solution.py:378
  429.1 7.7 %collective-permute-start.39 = (bf16[48,768]{1,0:T(8,128)(2,1)S(1)}, bf16[48,768]{1,0:T(8,128)(2,1)S(1)}, u32[]{:S(2)}, u32[]{:S(2)}) collective-permute-start(bf16[48,768]{1,0:T(8,128)(2,1)S(1)} %get-tuple-element.136), channel_id=1, source_target_pairs={{0,2},{1,3},{2,0},{3,1},{4,6},{5,7},{6,4},{7,5},{8,10},{9,11},{10,... | collective-permute-start | bytes 221192 | tf_op jit(solution)/shard_map/ppermute | solution.py:374
  431.6 7.0 %collective-permute-start.38 = (bf16[48,768]{1,0:T(8,128)(2,1)S(1)}, bf16[48,768]{1,0:T(8,128)(2,1)S(1)}, u32[]{:S(2)}, u32[]{:S(2)}) collective-permute-start(bf16[48,768]{1,0:T(8,128)(2,1)S(1)} %get-tuple-element.134), channel_id=1, source_target_pairs={{0,1},{1,2},{2,3},{3,0},{4,5},{5,6},{6,7},{7,4},{8,9},{9,10},{10,1... | collective-permute-start | bytes 221192 | tf_op jit(solution)/shard_map/ppermute | solution.py:374
  433.6 47.3 %collective-permute-start.29 = (bf16[256,576]{1,0:T(8,128)(2,1)S(1)}, bf16[256,576]{1,0:T(8,128)(2,1)S(1)}, u32[]{:S(2)}, u32[]{:S(2)}) collective-permute-start(bf16[256,576]{1,0:T(8,128)(2,1)S(1)} %get-tuple-element.68), channel_id=1, source_target_pairs={{0,3},{1,0},{2,1},{3,2},{4,7},{5,4},{6,5},{7,6},{8,11},{9,8},{10,9... | collective-permute-start | bytes 884744 | tf_op jit(solution)/shard_map/ppermute | solution.py:374
  443.8 7.9 %collective-permute-start.34 = (bf16[48,576]{1,0:T(8,128)(2,1)S(1)}, bf16[48,576]{1,0:T(8,128)(2,1)S(1)}, u32[]{:S(2)}, u32[]{:S(2)}) collective-permute-start(bf16[48,576]{1,0:T(8,128)(2,1)S(1)} %get-tuple-element.141), channel_id=1, source_target_pairs={{0,2},{1,3},{2,0},{3,1},{4,6},{5,7},{6,4},{7,5},{8,10},{9,11},{10,... | collective-permute-start | bytes 165896 | tf_op jit(solution)/shard_map/ppermute | solution.py:374
  (46 other events, 511.1 us)
Sparse Core Ops, SparseCore 0:
  19.3 76.5 all-gather.2
  241.9 86.7 all-gather.4
